TPU v7x, 32 devices: a whole 2x2x4 slice. The times are simulated.
32 devices in a mesh: basis: 4 (over y, x), docs: 8 (over z, core).
Axes of the slice: x: 2, y: 2, z: 4, core: 2. Of those that a mesh axis runs over, the one named last changes fastest.
Arguments:
- eig_in: bfloat16 [28672, 28672], P('basis', 'docs'), may hold values from -0.03125 to 0.03125
- eig_out: bfloat16 [8192, 8192], P('basis', 'docs'), may hold values from -0.0625 to 0.0625
- eigvals: bfloat16 [8192, 28672], P('basis', 'docs'), may hold values from 0.0025 to 3.6
- out_factors: bfloat16 [8192, 256], P('docs'), may hold values from -1.1953125 to 1.1953125
- in_factors: bfloat16 [28672, 256], P(('basis', 'docs')), may hold values from -1.1953125 to 1.1953125
- test_matrix: bfloat16 [28672, 32], P('docs'), may hold values from -0.03125 to 0.03125
- activations: bfloat16 [1024, 28672], P('docs', 'basis'), may hold values from -6 to 6
- gradients: bfloat16 [1024, 8192], P('docs', 'basis'), may hold values from -0.00059890747 to 0.00059890747
- doc_lengths: int32 [32], replicated, may hold values from 1 to 96, 1024 in all
Outputs:
- scores: float32 [1024, 4], P('docs')
- doc_influence: float32 [32, 4], replicated
Inputs may be any that keep to these rules, and one draw needn't show every extreme that they name: `doc_lengths`: the documents lie end to end in token order and their lengths sum to 1024.
All inputs are finite; a program needn't handle non-finite values.
Results may differ from a plain program's by a relative error of at most 0.0085.
Values may be sent and summed in bfloat16 or wider, within the bound.
No kernel may reach another device: no remote copies, remote signals or barrier semaphores. Data moves between devices by JAX's collectives and lax.ppermute only.
A program may use at most 320 MiB of HBM per device.

v0:
```python
import functools

import jax
import jax.numpy as jnp
import numpy as np
from jax import lax
from jax.experimental import pallas as pl
from jax.experimental.pallas import tpu as pltpu
from jax.sharding import PartitionSpec as P

QUERIES = 4
LQ = 64
RANK = 32
CORES = 2
VMEM = 56 * 1024 * 1024

damping = 0.1
highest = lax.Precision.HIGHEST
f32 = jnp.float32
bf16 = jnp.bfloat16


def tile(extent, most, unit):
    best = extent
    for size in range(unit, min(most, extent) + 1, unit):
        if extent % size == 0:
            best = size
    return best


def params():
    return pltpu.CompilerParams(vmem_limit_bytes=VMEM)


def hold(x, *others):
    others = [other[:16, :128] for other in others]
    return pl.pallas_call(
        lambda *refs: None,
        out_shape=jax.ShapeDtypeStruct(x.shape, x.dtype),
        in_specs=[pl.BlockSpec(memory_space=pl.ANY)] * (1 + len(others)),
        out_specs=pl.BlockSpec(memory_space=pl.ANY),
        input_output_aliases={0: 0},
        name="hold",
    )(x, *others)


def xor_permute(x, axis, size, bits):
    return lax.ppermute(x, axis, [(i, i ^ bits) for i in range(size)])


def tree_sum(parts):
    while len(parts) > 1:
        parts = [parts[i] + parts[i + 1] for i in range(0, len(parts), 2)]
    return parts[0]


def in_order(parts, me):
    bit = 1
    while bit < len(parts):
        on = (me & bit) != 0
        parts = [jnp.where(on, parts[s ^ bit], parts[s]) for s in range(len(parts))]
        bit *= 2
    return parts


def scatter_direct(x, axis, size, me, unit, dim, kind):
    chunk = x.shape[dim] // size
    total = lax.dynamic_slice_in_dim(x, me * chunk, chunk, dim).astype(f32)
    low = x.astype(kind)
    whole = lax.axis_size(axis)
    for s in range(1, size):
        piece = lax.dynamic_slice_in_dim(low, (me ^ s) * chunk, chunk, dim)
        total = total + xor_permute(piece, axis, whole, unit * s).astype(f32)
    return total


def gather_direct(y, axis, size, me, unit, dim):
    whole = lax.axis_size(axis)
    parts = [y] + [xor_permute(y, axis, whole, unit * s) for s in range(1, size)]
    return jnp.concatenate(in_order(parts, me), axis=dim)


def reduce_basis(x, dim):
    size = lax.axis_size("basis")
    me = lax.axis_index("basis")
    mine = scatter_direct(x, "basis", size, me, 1, dim, bf16).astype(bf16)
    return gather_direct(mine, "basis", size, me, 1, dim)


def halve_basis(x, bits):
    size = lax.axis_size("basis")
    me = lax.axis_index("basis")
    for n, bit in enumerate(bits):
        half = x.shape[0] // 2
        on = (me & bit) // bit
        kept = lax.dynamic_slice_in_dim(x, on * half, half, 0)
        given = lax.dynamic_slice_in_dim(x, (1 - on) * half, half, 0)
        x = kept + xor_permute(given.astype(f32 if n else bf16), "basis", size, bit).astype(f32)
    x = x.astype(bf16)
    for bit in bits[::-1]:
        on = (me & bit) // bit
        late = x
        x = jnp.concatenate(in_order([x, xor_permute(x, "basis", size, bit)], on), axis=0)
    return x, late


def reduce_rotated(x):
    bits = []
    while 1 << len(bits) < lax.axis_size("basis"):
        bits.append(1 << len(bits))
    half = x.shape[0] // 2
    upper, _ = halve_basis(x[:half], bits)
    lower, late = halve_basis(x[half:], bits[::-1])
    return jnp.concatenate([upper, lower], axis=0), late


def scatter_docs(x, dim, near, far):
    size = lax.axis_size("docs")
    me = lax.axis_index("docs")
    core, place = me % CORES, me // CORES
    half = x.shape[dim] // CORES
    kept = lax.dynamic_slice_in_dim(x, core * half, half, dim).astype(f32)
    given = lax.dynamic_slice_in_dim(x, (1 - core) * half, half, dim).astype(near)
    chip = kept + xor_permute(given, "docs", size, 1).astype(f32)
    return scatter_direct(chip, "docs", size // CORES, place, CORES, dim, far).astype(bf16)


def gather_docs(mine, dim):
    size = lax.axis_size("docs")
    me = lax.axis_index("docs")
    core, place = me % CORES, me // CORES
    ours = gather_direct(mine, "docs", size // CORES, place, CORES, dim)
    theirs = xor_permute(ours, "docs", size, 1)
    return jnp.concatenate(in_order([ours, theirs], core), axis=dim)


def regroup_near(x):
    size = lax.axis_size("docs")
    core = lax.axis_index("docs") % CORES
    half = x.shape[1] // CORES
    kept = lax.dynamic_slice_in_dim(x, core * half, half, 1)
    given = lax.dynamic_slice_in_dim(x, (1 - core) * half, half, 1)
    return jnp.concatenate(in_order([kept, xor_permute(given, "docs", size, 1)], core), axis=0)


def regroup_far(x):
    size = lax.axis_size("docs")
    places = size // CORES
    place = lax.axis_index("docs") // CORES
    chunk = x.shape[1] // places
    parts = [lax.dynamic_slice_in_dim(x, place * chunk, chunk, 1)]
    for s in range(1, places):
        piece = lax.dynamic_slice_in_dim(x, (place ^ s) * chunk, chunk, 1)
        parts.append(xor_permute(piece, "docs", size, CORES * s))
    return parts


def own_tokens(x):
    size = lax.axis_size("docs")
    me = lax.axis_index("docs")
    core, place = me % CORES, me // CORES
    places = size // CORES
    x = x.reshape(places, CORES, x.shape[0] // size, x.shape[1])
    kept = lax.dynamic_index_in_dim(x, core, 1, keepdims=False)
    given = lax.dynamic_index_in_dim(x, 1 - core, 1, keepdims=False)
    chip = kept + xor_permute(given, "docs", size, 1)
    return scatter_direct(chip, "docs", places, place, CORES, 0, f32)[0]


def spread_left(block):
    size = lax.axis_size("docs")
    places = size // CORES
    me = lax.axis_index("docs") // CORES
    here = lax.axis_index("basis")
    left = jnp.where(me == here, block, jnp.zeros_like(block))
    for s in range(1, places):
        pairs = [
            (b * size + b * CORES + c, b * size + (b ^ s) * CORES + c)
            for b in range(places)
            for c in range(CORES)
        ]
        left = left + lax.ppermute(block, ("basis", "docs"), pairs)
    return left


def join_cores(x):
    size = lax.axis_size("docs")
    core = lax.axis_index("docs") % CORES
    return jnp.concatenate(in_order([x, xor_permute(x, "docs", size, 1)], core), axis=1)


def moment_kernel(width, out_ref, in_ref, values_ref, test_ref, *refs):
    moment_refs, sketch_ref = refs[:QUERIES], refs[QUERIES]
    rows, cols = values_ref.shape
    sides = [out_ref[:, q * LQ : (q + 1) * LQ] for q in range(QUERIES)]

    def step(c, carry):
        at = pl.ds(pl.multiple_of(c * width, width), width)
        weight = 1.0 / (values_ref[:, at].astype(f32) + damping)
        for q in range(QUERIES):
            product = jnp.dot(
                sides[q], in_ref[q * LQ : (q + 1) * LQ, at], preferred_element_type=f32
            )
            moment_refs[q][:, at] = (product * weight).astype(bf16)
        return carry

    lax.fori_loop(0, cols // width, step, 0)
    for q in range(QUERIES):
        sketch_ref[q * RANK : (q + 1) * RANK, :] = lax.dot_general(
            test_ref[...],
            moment_refs[q][...],
            (((1,), (1,)), ((), ())),
            preferred_element_type=f32,
        )


def moment_pass(rot_out, rot_in, eigvals, test):
    rows, cols = eigvals.shape
    height = tile(rows, 256, 128)
    width = tile(cols, 512, 128)
    *moments, sketch = pl.pallas_call(
        functools.partial(moment_kernel, width),
        out_shape=[jax.ShapeDtypeStruct((rows, cols), bf16)] * QUERIES
        + [jax.ShapeDtypeStruct((QUERIES * RANK, rows), f32)],
        grid=(rows // height,),
        in_specs=[
            pl.BlockSpec((height, rot_out.shape[1]), lambda i: (i, 0)),
            pl.BlockSpec(rot_in.shape, lambda i: (0, 0)),
            pl.BlockSpec((height, cols), lambda i: (i, 0)),
            pl.BlockSpec(test.shape, lambda i: (0, 0)),
        ],
        out_specs=[pl.BlockSpec((height, cols), lambda i: (i, 0))] * QUERIES
        + [pl.BlockSpec((QUERIES * RANK, height), lambda i: (0, i))],
        compiler_params=params(),
        cost_estimate=pl.CostEstimate(
            flops=4 * 2 * QUERIES * rows * cols * 256,
            bytes_accessed=QUERIES * rows * cols * 2 + rows * cols * 2,
            transcendentals=0,
        ),
        name="moment_pass",
    )(rot_out, rot_in, eigvals, test)
    return moments, sketch


def cross_kernel(sketch_ref, *refs):
    cross_ref = refs[QUERIES]
    for q in range(QUERIES):
        cross_ref[q * RANK : (q + 1) * RANK, :] = jnp.dot(
            sketch_ref[q * RANK : (q + 1) * RANK, :], refs[q][...], preferred_element_type=f32
        )


def cross_pass(sketch, moments):
    rows, cols = moments[0].shape
    width = tile(cols, 512, 128)
    return pl.pallas_call(
        cross_kernel,
        out_shape=jax.ShapeDtypeStruct((QUERIES * RANK, cols), f32),
        grid=(cols // width,),
        in_specs=[pl.BlockSpec(sketch.shape, lambda j: (0, 0))]
        + [pl.BlockSpec((rows, width), lambda j: (0, j))] * QUERIES,
        out_specs=pl.BlockSpec((QUERIES * RANK, width), lambda j: (0, j)),
        compiler_params=params(),
        cost_estimate=pl.CostEstimate(
            flops=2 * QUERIES * rows * cols * 256,
            bytes_accessed=QUERIES * rows * cols * 2,
            transcendentals=0,
        ),
        name="cross_pass",
    )(sketch, *moments)


def inverse_kernel(gram_ref, out_ref):
    gram = gram_ref[...]
    row = lax.broadcasted_iota(jnp.int32, gram.shape, 1)
    col = lax.broadcasted_iota(jnp.int32, gram.shape, 2)
    unit = jnp.where(row == col, 1.0, 0.0).astype(f32)
    below = lax.broadcasted_iota(jnp.int32, (gram.shape[0], RANK, 1), 1)
    for k in range(RANK):
        pivot = gram[:, k : k + 1, k : k + 1]
        factor = jnp.where(below > k, gram[:, :, k : k + 1] / pivot, 0.0)
        unit = unit - factor * unit[:, k : k + 1, :]
        gram = gram - factor * gram[:, k : k + 1, :]
    diagonal = jnp.sum(jnp.where(row == col, gram, 0.0), axis=2, keepdims=True)
    out_ref[...] = unit / jnp.sqrt(diagonal)


def inverse_factor(gram):
    return pl.pallas_call(
        inverse_kernel,
        out_shape=jax.ShapeDtypeStruct(gram.shape, f32),
        compiler_params=params(),
        name="inverse_factor",
    )(gram)


def right_kernel(parts, *refs):
    projected_ref, out_ref, across_ref = refs[parts:]

    @pl.when(pl.program_id(0) == 0)
    def _():
        across_ref[...] = jnp.transpose(projected_ref[...].astype(f32)).astype(bf16)

    height = refs[0].shape[0]
    for n in range(parts):
        out_ref[n * height : (n + 1) * height, :] = jnp.dot(
            refs[n][...], across_ref[...], preferred_element_type=f32
        ).astype(out_ref.dtype)


def right_pass(eig_in, projected):
    rows, cols = eig_in.shape
    parts = 4
    height = tile(rows // parts, 256, 16)
    width = projected.shape[0]
    return pl.pallas_call(
        functools.partial(right_kernel, parts),
        out_shape=jax.ShapeDtypeStruct((rows, width), bf16),
        grid=(rows // (parts * height),),
        in_specs=[
            pl.BlockSpec((height, cols), lambda i, n=n: (parts * i + n, 0)) for n in range(parts)
        ]
        + [pl.BlockSpec(projected.shape, lambda i: (0, 0))],
        out_specs=pl.BlockSpec((parts * height, width), lambda i: (i, 0)),
        scratch_shapes=[pltpu.VMEM(projected.shape[::-1], bf16)],
        compiler_params=params(),
        cost_estimate=pl.CostEstimate(
            flops=2 * rows * cols * 256,
            bytes_accessed=rows * cols * 2,
            transcendentals=0,
        ),
        name="right_pass",
    )(*[eig_in] * parts, projected)


def rotate_in(eig_in, in_factors, ready):
    size = lax.axis_size("docs")
    places = size // CORES
    me = lax.axis_index("docs")
    core, place = me % CORES, me // CORES
    chunks = [in_factors]
    depth = CORES * in_factors.shape[0]
    totals = []
    for s in range(places):
        if s > 0:
            low = s & -s
            chunks.append(xor_permute(chunks[s - low], "docs", size, CORES * low))
    for s, chunk in enumerate(chunks):
        if s > 1:
            chunk = hold(chunk, totals[1])
        mate = xor_permute(chunk, "docs", size, 1)
        if s == places - 1:
            ready = hold(ready, totals[s - 1])
            mate = hold(mate, ready)
        both = jnp.concatenate(in_order([chunk, mate], core), axis=0)
        rows = lax.dynamic_slice_in_dim(eig_in, (place ^ s) * depth, depth, 0)
        product = lax.dot_general(
            both, rows, (((0,), (0,)), ((), ())), preferred_element_type=f32
        )
        totals.append(totals[-1] + product if totals else product)
    return totals[-1], ready


def local(
    eig_in,
    eig_out,
    eigvals,
    out_factors,
    in_factors,
    test_matrix,
    activations,
    gradients,
    doc_lengths,
):
    cols_in = eig_in.shape[1]
    tok_count = activations.shape[0]
    basis = lax.axis_size("basis")
    docs = lax.axis_size("docs")

    part_out = jnp.dot(eig_out, out_factors, preferred_element_type=f32)
    mine_out = scatter_docs(part_out, 0, f32, bf16)
    part_in, mine_out = rotate_in(eig_in, in_factors, mine_out)
    rot_out = gather_docs(hold(mine_out, part_in), 0)
    rot_in, late = reduce_rotated(part_in)

    moments, part = moment_pass(rot_out, rot_in, eigvals, jnp.transpose(test_matrix))
    all_tokens = regroup_far(hold(regroup_near(activations), late))
    part = hold(part, *all_tokens[1:])
    sketch = gather_docs(scatter_docs(part, 1, f32, bf16), 1)
    split = sketch.reshape(QUERIES, RANK, sketch.shape[1])
    gram = jnp.einsum("qri,qsi->qrs", split, split, preferred_element_type=f32)
    gram = tree_sum([gram] + [xor_permute(gram, "basis", basis, s) for s in range(1, basis)])
    cross = cross_pass(sketch, moments)
    back = jnp.dot(sketch, eig_out, preferred_element_type=f32)
    inverse = inverse_factor(gram)
    both = jnp.concatenate([cross, back], axis=1)
    solved = jnp.einsum(
        "qkr,qrj->qkj",
        inverse,
        both.reshape(QUERIES, RANK, both.shape[1]),
        precision=highest,
        preferred_element_type=f32,
    ).reshape(both.shape)
    solved = reduce_basis(solved, 0)
    projected = solved[:, :cols_in]
    left = spread_left(solved[:, cols_in:])
    right = hold(right_pass(eig_in, projected), left)
    token_out = lax.dot_general(
        gradients, join_cores(left), (((1,), (1,)), ((), ())), preferred_element_type=f32
    )
    right = scatter_docs(right, 0, bf16, bf16)
    all_tokens = jnp.concatenate(in_order(all_tokens, lax.axis_index("docs") // CORES), axis=0)
    token_in = own_tokens(jnp.dot(all_tokens, right, preferred_element_type=f32))

    tokens = jnp.concatenate([token_in, token_out], axis=1)
    tokens = tree_sum(
        [tokens] + [xor_permute(tokens, "basis", basis, s) for s in range(1, basis)]
    )
    width = QUERIES * RANK
    scores = (tokens[:, :width] * tokens[:, width:]).reshape(tok_count, QUERIES, RANK).sum(axis=2)
    positions = lax.axis_index("docs") * tok_count + jnp.arange(tok_count, dtype=jnp.int32)
    doc_ends = jnp.cumsum(doc_lengths)
    doc_starts = doc_ends - doc_lengths
    member = (
        (positions[:, None] >= doc_starts[None, :]) & (positions[:, None] < doc_ends[None, :])
    ).astype(f32)
    doc_part = lax.dot_general(member, scores, (((0,), (0,)), ((), ())), precision=highest)
    doc_part = doc_part + xor_permute(doc_part, "docs", docs, 1)
    doc_influence = tree_sum(
        [doc_part]
        + [xor_permute(doc_part, "docs", docs, CORES * s) for s in range(1, docs // CORES)]
    )
    return (scores, doc_influence)


def solution(mesh):
    return jax.shard_map(
        local,
        mesh=mesh,
        in_specs=(
            P("basis", "docs"),
            P("basis", "docs"),
            P("basis", "docs"),
            P("docs", None),
            P(("basis", "docs"), None),
            P("docs", None),
            P("docs", "basis"),
            P("docs", "basis"),
            P(),
        ),
        out_specs=(P("docs", None), P()),
        check_vma=False,
    )
```

profile of v0, /device:TPU:0, one launch (start us, length us, event | category | flops | bytes accessed | tf_op | source)
XLA Modules:
  0.0 373.6 jit_solution(11535829729699179199)
XLA Ops:
  1.2 3.7 collective-permute-start.4
  13.6 12.5 %collective-permute-done.4.refs_0_ = bf16[896,256]{1,0:T(8,128)(2,1)S(1)} collective-permute-done((bf16[896,256]{1,0:T(8,128)(2,1)}, bf16[896,256]{1,0:T(8,128)(2,1)S(1)}, u32[]{:S(2)}, u32[]{:S(2)}) %collective-permute-start.4) | collective-permute-done | bytes 458784 | tf_op jit(solution)/shard_map/ppermute | solution.py:48
  27.9 6.6 %fusion.6 = f32[256,3584]{1,0:T(8,128)S(1)} fusion(bf16[7168,3584]{1,0:T(8,128)(2,1)} %refs_3_.1, s32[]{:T(128)S(6)} %select_n.456, bf16[896,256]{1,0:T(8,128)(2,1)S(1)} %get-tuple-element.52, bf16[896,256]{1,0:T(8,128)(2,1)S(1)} %get-tuple-element.51), kind=kOutput, calls=%fused_computation.6 | convolution fusion | flops 3290169344 | bytes 17432580 | tf_op jit(solution)/shard_map/dot_general | solution.py:357
  35.6 6.6 %fusion.8 = f32[256,3584]{1,0:T(8,128)S(1)} fusion(f32[256,3584]{1,0:T(8,128)S(1)} %fusion.6, bf16[7168,3584]{1,0:T(8,128)(2,1)} %refs_3_.1, s32[]{:T(128)S(6)} %select_n.459, bf16[896,256]{1,0:T(8,128)(2,1)S(1)} %get-tuple-element.50, bf16[896,256]{1,0:T(8,128)(2,1)S(1)} %get-tuple-element.49), kind=kOutput, calls=%fused_computation.8 | convolution fusion | flops 3291086848 | bytes 21102596 | tf_op jit(solution)/shard_map/dot_general | solution.py:357
  55.4 5.9 %collective-permute-done.11 = bf16[256,256]{1,0:T(8,128)(2,1)S(1)} collective-permute-done((bf16[256,256]{1,0:T(8,128)(2,1)S(1)}, bf16[256,256]{1,0:T(8,128)(2,1)S(1)}, u32[]{:S(2)}, u32[]{:S(2)}) %collective-permute-start.11) | collective-permute-done | bytes 131104 | tf_op jit(solution)/shard_map/ppermute | solution.py:48
  61.3 3.9 %collective-permute-done.10 = bf16[256,256]{1,0:T(8,128)(2,1)S(1)} collective-permute-done((bf16[256,256]{1,0:T(8,128)(2,1)S(1)}, bf16[256,256]{1,0:T(8,128)(2,1)S(1)}, u32[]{:S(2)}, u32[]{:S(2)}) %collective-permute-start.10) | collective-permute-done | bytes 131104 | tf_op jit(solution)/shard_map/ppermute | solution.py:48
  67.0 6.9 %fusion.11 = f32[256,3584]{1,0:T(8,128)S(1)} fusion(f32[256,3584]{1,0:T(8,128)S(1)} %copy-done.20, bf16[7168,3584]{1,0:T(8,128)(2,1)} %refs_3_.1, s32[]{:T(128)S(6)} %select_n.462, bf16[896,256]{1,0:T(8,128)(2,1)S(1)} %get-tuple-element.48, bf16[896,256]{1,0:T(8,128)(2,1)S(1)} %get-tuple-element.47), kind=kOutput, calls=%fused_computation.9 | convolution fusion | flops 3291086848 | bytes 21102596 | tf_op jit(solution)/shard_map/dot_general | solution.py:357
  79.4 9.3 %fusion.14 = f32[256,3584]{1,0:T(8,128)S(1)} fusion(f32[256,3584]{1,0:T(8,128)} %copy-done.21, bf16[7168,3584]{1,0:T(8,128)(2,1)} %refs_3_.1, s32[]{:T(128)S(6)} %select_n.471, bf16[896,256]{1,0:T(8,128)(2,1)S(1)} %get-tuple-element.46, bf16[896,256]{1,0:T(8,128)(2,1)S(1)} %get-tuple-element.45), kind=kOutput, calls=%fused_computation.10 | convolution fusion | flops 3291086848 | bytes 21102596 | tf_op jit(solution)/shard_map/dot_general | solution.py:357
  99.6 4.0 %collective-permute-done.19 = bf16[256,256]{1,0:T(8,128)(2,1)S(1)} collective-permute-done((bf16[256,256]{1,0:T(8,128)(2,1)}, bf16[256,256]{1,0:T(8,128)(2,1)S(1)}, u32[]{:S(2)}, u32[]{:S(2)}) %collective-permute-start.19) | collective-permute-done | bytes 131104 | tf_op jit(solution)/shard_map/ppermute | solution.py:48
  112.1 6.5 %collective-permute-done.13 = f32[32,3584]{1,0:T(8,128)S(1)} collective-permute-done((f32[32,3584]{1,0:T(8,128)S(1)}, f32[32,3584]{1,0:T(8,128)S(1)}, u32[]{:S(2)}, u32[]{:S(2)}) %collective-permute-start.13) | collective-permute-done | bytes 458784 | tf_op jit(solution)/shard_map/ppermute | solution.py:48
  138.4 44.5 %moment_pass.1 = (bf16[2048,3584]{1,0:T(8,128)(2,1)}, bf16[2048,3584]{1,0:T(8,128)(2,1)}, bf16[2048,3584]{1,0:T(8,128)(2,1)}, bf16[2048,3584]{1,0:T(8,128)(2,1)}, f32[128,2048]{1,0:T(8,128)}) custom-call(bf16[2048,256]{1,0:T(8,128)(2,1)} %pad_maximum_fusion.4.out_ref, bf16[256,3584]{1,0:T(8,128)(2,1)} %pad_maximum_fusion.2.in_ref, ...), custom_call_target="tpu_custom_call" | custom-call | flops 60129542144 | bytes 73400320 | tf_op jit(solution)/shard_map/moment_pass/pallas_call | solution.py:221
  191.2 3.7 collective-permute-start.28
  197.3 4.2 %collective-permute-done.30 = bf16[128,256]{1,0:T(8,128)(2,1)S(1)} collective-permute-done((bf16[128,256]{1,0:T(8,128)(2,1)S(1)}, bf16[128,256]{1,0:T(8,128)(2,1)S(1)}, u32[]{:S(2)}, u32[]{:S(2)}) %collective-permute-start.30) | collective-permute-done | bytes 65568 | tf_op jit(solution)/shard_map/ppermute | solution.py:48
  221.1 22.4 %cross_pass.1 = f32[128,3584]{1,0:T(8,128)} custom-call(bf16[128,2048]{1,0:T(8,128)(2,1)} %copy-done.3, bf16[2048,3584]{1,0:T(8,128)(2,1)} %get-tuple-element.8.refs_0_, bf16[2048,3584]{1,0:T(8,128)(2,1)} %get-tuple-element.9.refs_1_, bf16[2048,3584]{1,0:T(8,128)(2,1)} %get-tuple-element.10.refs_2_, bf16[2048,3584]{1,0:T(8,128)(2,1)} %get-tuple-element.11.refs_3_), custom_call_target="tpu_custom_call" | custom-call | flops 15032385536 | bytes 58720256 | tf_op jit(solution)/shard_map/cross_pass/pallas_call | solution.py:256
  245.8 4.1 %inverse_factor.1 = f32[4,32,32]{2,1,0:T(8,128)} custom-call(f32[4,32,32]{2,1,0:T(8,128)} %add_add_fusion.2.gram_ref), custom_call_target="tpu_custom_call" | custom-call | tf_op jit(solution)/shard_map/inverse_factor/pallas_call | solution.py:289
  256.7 6.6 %collective-permute-done.38 = bf16[32,4608]{1,0:T(8,128)(2,1)} collective-permute-done((bf16[32,4608]{1,0:T(8,128)(2,1)S(1)}, bf16[32,4608]{1,0:T(8,128)(2,1)}, u32[]{:S(2)}, u32[]{:S(2)}) %collective-permute-start.38) | collective-permute-done | bytes 294944 | tf_op jit(solution)/shard_map/ppermute | solution.py:48
  263.3 4.8 %collective-permute-done.40 = bf16[32,4608]{1,0:T(8,128)(2,1)} collective-permute-done((bf16[32,4608]{1,0:T(8,128)(2,1)S(1)}, bf16[32,4608]{1,0:T(8,128)(2,1)}, u32[]{:S(2)}, u32[]{:S(2)}) %collective-permute-start.40) | collective-permute-done | bytes 294944 | tf_op jit(solution)/shard_map/ppermute | solution.py:48
  274.2 5.5 %collective-permute-done.43 = bf16[32,4608]{1,0:T(8,128)(2,1)S(1)} collective-permute-done((bf16[32,4608]{1,0:T(8,128)(2,1)S(1)}, bf16[32,4608]{1,0:T(8,128)(2,1)S(1)}, u32[]{:S(2)}, u32[]{:S(2)}) %collective-permute-start.43) | collective-permute-done | bytes 294944 | tf_op jit(solution)/shard_map/ppermute | solution.py:48
  279.7 4.3 %collective-permute-done.42 = bf16[32,4608]{1,0:T(8,128)(2,1)S(1)} collective-permute-done((bf16[32,4608]{1,0:T(8,128)(2,1)S(1)}, bf16[32,4608]{1,0:T(8,128)(2,1)S(1)}, u32[]{:S(2)}, u32[]{:S(2)}) %collective-permute-start.42) | collective-permute-done | bytes 294944 | tf_op jit(solution)/shard_map/ppermute | solution.py:48
  284.2 3.7 collective-permute-start.46
  291.6 23.1 %right_pass.1.refs_0_ = bf16[7168,128]{1,0:T(8,128)(2,1)} custom-call(bf16[7168,3584]{1,0:T(8,128)(2,1)} %refs_3_.1, bf16[7168,3584]{1,0:T(8,128)(2,1)} %refs_3_.1, bf16[7168,3584]{1,0:T(8,128)(2,1)} %refs_3_.1, bf16[7168,3584]{1,0:T(8,128)(2,1)} %refs_3_.1, bf16[128,3584]{1,0:T(8,128)(2,1)} %slice.71.refs_4_), custom_call_target="tpu_custom_call" | custom-call | flops 13153337344 | bytes 51380224 | tf_op jit(solution)/shard_map/right_pass/pallas_call | solution.py:316
  325.8 7.5 %collective-permute-done.48 = bf16[896,128]{1,0:T(8,128)(2,1)S(1)} collective-permute-done((bf16[896,128]{1,0:T(8,128)(2,1)S(1)}, bf16[896,128]{1,0:T(8,128)(2,1)S(1)}, u32[]{:S(2)}, u32[]{:S(2)}) %collective-permute-start.48) | collective-permute-done | bytes 229408 | tf_op jit(solution)/shard_map/ppermute | solution.py:48
  333.2 11.0 %collective-permute-done.49 = bf16[896,128]{1,0:T(8,128)(2,1)S(1)} collective-permute-done((bf16[896,128]{1,0:T(8,128)(2,1)S(1)}, bf16[896,128]{1,0:T(8,128)(2,1)S(1)}, u32[]{:S(2)}, u32[]{:S(2)}) %collective-permute-start.49) | collective-permute-done | bytes 229408 | tf_op jit(solution)/shard_map/ppermute | solution.py:48
  360.3 3.5 collective-permute-done.57
  (251 shorter events, 157.7 us)
Async XLA Ops:
  0.6 26.2 %collective-permute-start.1 = (bf16[896,256]{1,0:T(8,128)(2,1)}, bf16[896,256]{1,0:T(8,128)(2,1)}, u32[]{:S(2)}, u32[]{:S(2)}) collective-permute-start(bf16[896,256]{1,0:T(8,128)(2,1)} %param.13), channel_id=1, source_target_pairs={{0,1},{1,0},{2,3},{3,2},{4,5},{5,4},{6,7},{7,6},{8,9},{9,8},{10,11... | collective-permute-start | bytes 1376264 | tf_op jit(solution)/shard_map/ppermute | solution.py:48
  1.2 24.9 %collective-permute-start.4 = (bf16[896,256]{1,0:T(8,128)(2,1)}, bf16[896,256]{1,0:T(8,128)(2,1)S(1)}, u32[]{:S(2)}, u32[]{:S(2)}) collective-permute-start(bf16[896,256]{1,0:T(8,128)(2,1)} %param.13), channel_id=1, source_target_pairs={{0,4},{1,5},{2,6},{3,7},{4,0},{5,1},{6,2},{7,3},{8,12},{9,13},{10,... | collective-permute-start | bytes 1376264 | tf_op jit(solution)/shard_map/ppermute | solution.py:48
  4.8 22.0 %collective-permute-start.2 = (bf16[896,256]{1,0:T(8,128)(2,1)}, bf16[896,256]{1,0:T(8,128)(2,1)}, u32[]{:S(2)}, u32[]{:S(2)}) collective-permute-start(bf16[896,256]{1,0:T(8,128)(2,1)} %param.13), channel_id=1, source_target_pairs={{0,2},{1,3},{2,0},{3,1},{4,6},{5,7},{6,4},{7,5},{8,10},{9,11},{10,... | collective-permute-start | bytes 1376264 | tf_op jit(solution)/shard_map/ppermute | solution.py:48
  8.6 37.4 %collective-permute-start = (bf16[128,3584]{1,0:T(8,128)(2,1)}, bf16[128,3584]{1,0:T(8,128)(2,1)}, u32[]{:S(2)}, u32[]{:S(2)}) collective-permute-start(bf16[128,3584]{1,0:T(8,128)(2,1)} %constant_dynamic-slice_fusion.25), channel_id=1, source_target_pairs={{0,1},{1,0},{2,3},{3,2},{4,5},{5,4},{6,7},{7,6},{8,9},{9,8},{10,11... | collective-permute-start | bytes 2752520 | tf_op jit(solution)/shard_map/ppermute | solution.py:48
  13.1 34.6 %collective-permute-start.8 = (f32[1024,256]{1,0:T(8,128)}, f32[1024,256]{1,0:T(8,128)}, u32[]{:S(2)}, u32[]{:S(2)}) collective-permute-start(f32[1024,256]{1,0:T(8,128)} %constant_dynamic-slice_fusion.24), channel_id=1, source_target_pairs={{0,1},{1,0},{2,3},{3,2},{4,5},{5,4},{6,7},{7,6},{8,9},{9,8},{10,11... | collective-permute-start | bytes 3145736 | tf_op jit(solution)/shard_map/ppermute | solution.py:48
  26.1 18.6 %collective-permute-start.6 = (bf16[896,256]{1,0:T(8,128)(2,1)S(1)}, bf16[896,256]{1,0:T(8,128)(2,1)S(1)}, u32[]{:S(2)}, u32[]{:S(2)}) collective-permute-start(bf16[896,256]{1,0:T(8,128)(2,1)S(1)} %collective-permute-done.4.refs_0_), channel_id=1, source_target_pairs={{0,2},{1,3},{2,0},{3,1},{4,6},{5,7},{6,4},{7,5},{8,10},{9,11},{10,... | collective-permute-start | bytes 1376264 | tf_op jit(solution)/shard_map/ppermute | solution.py:48
  44.7 21.2 %collective-permute-start.5 = (bf16[896,256]{1,0:T(8,128)(2,1)}, bf16[896,256]{1,0:T(8,128)(2,1)}, u32[]{:S(2)}, u32[]{:S(2)}) collective-permute-start(bf16[896,256]{1,0:T(8,128)(2,1)} %hold.8), channel_id=1, source_target_pairs={{0,1},{1,0},{2,3},{3,2},{4,5},{5,4},{6,7},{7,6},{8,9},{9,8},{10,11... | collective-permute-start | bytes 1376264 | tf_op jit(solution)/shard_map/ppermute | solution.py:48
  45.5 32.1 %collective-permute-start.7 = (bf16[896,256]{1,0:T(8,128)(2,1)}, bf16[896,256]{1,0:T(8,128)(2,1)S(1)}, u32[]{:S(2)}, u32[]{:S(2)}) collective-permute-start(bf16[896,256]{1,0:T(8,128)(2,1)} %hold.9), channel_id=1, source_target_pairs={{0,1},{1,0},{2,3},{3,2},{4,5},{5,4},{6,7},{7,6},{8,9},{9,8},{10,11... | collective-permute-start | bytes 1376264 | tf_op jit(solution)/shard_map/ppermute | solution.py:48
  90.8 12.8 %collective-permute-start.19 = (bf16[256,256]{1,0:T(8,128)(2,1)}, bf16[256,256]{1,0:T(8,128)(2,1)S(1)}, u32[]{:S(2)}, u32[]{:S(2)}) collective-permute-start(bf16[256,256]{1,0:T(8,128)(2,1)} %hold.13), channel_id=1, source_target_pairs={{0,4},{1,5},{2,6},{3,7},{4,0},{5,1},{6,2},{7,3},{8,12},{9,13},{10,... | collective-permute-start | bytes 393224 | tf_op jit(solution)/shard_map/ppermute | solution.py:48
  129.8 53.1 %collective-permute-start.15 = (bf16[256,896]{1,0:T(8,128)(2,1)S(1)}, bf16[256,896]{1,0:T(8,128)(2,1)S(1)}, u32[]{:S(2)}, u32[]{:S(2)}) collective-permute-start(bf16[256,896]{1,0:T(8,128)(2,1)S(1)} %get-tuple-element.26), channel_id=1, source_target_pairs={{0,6},{1,7},{2,4},{3,5},{4,2},{5,3},{6,0},{7,1},{8,14},{9,15},{10,... | collective-permute-start | bytes 1376264 | tf_op jit(solution)/shard_map/ppermute | solution.py:48
  132.0 52.2 %collective-permute-start.17 = (bf16[256,896]{1,0:T(8,128)(2,1)S(1)}, bf16[256,896]{1,0:T(8,128)(2,1)S(1)}, u32[]{:S(2)}, u32[]{:S(2)}) collective-permute-start(bf16[256,896]{1,0:T(8,128)(2,1)S(1)} %get-tuple-element.27), channel_id=1, source_target_pairs={{0,2},{1,3},{2,0},{3,1},{4,6},{5,7},{6,4},{7,5},{8,10},{9,11},{10,... | collective-permute-start | bytes 1376264 | tf_op jit(solution)/shard_map/ppermute | solution.py:48
  133.7 51.9 %collective-permute-start.16 = (bf16[256,896]{1,0:T(8,128)(2,1)S(1)}, bf16[256,896]{1,0:T(8,128)(2,1)S(1)}, u32[]{:S(2)}, u32[]{:S(2)}) collective-permute-start(bf16[256,896]{1,0:T(8,128)(2,1)S(1)} %get-tuple-element.28), channel_id=1, source_target_pairs={{0,4},{1,5},{2,6},{3,7},{4,0},{5,1},{6,2},{7,3},{8,12},{9,13},{10,... | collective-permute-start | bytes 1376264 | tf_op jit(solution)/shard_map/ppermute | solution.py:48
  217.6 27.5 %collective-permute-start.37 = (f32[4,32,32]{2,1,0:T(8,128)S(1)}, f32[4,32,32]{2,1,0:T(8,128)S(1)}, u32[]{:S(2)}, u32[]{:S(2)}) collective-permute-start(f32[4,32,32]{2,1,0:T(8,128)S(1)} %fusion.61), channel_id=1, source_target_pairs={{0,24},{8,16},{16,8},{24,0},{1,25},{9,17},{17,9},{25,1},{2,26},{10... | collective-permute-start | bytes 49160 | tf_op jit(solution)/shard_map/ppermute | solution.py:48
  219.1 26.1 %collective-permute-start.36 = (f32[4,32,32]{2,1,0:T(8,128)S(1)}, f32[4,32,32]{2,1,0:T(8,128)S(1)}, u32[]{:S(2)}, u32[]{:S(2)}) collective-permute-start(f32[4,32,32]{2,1,0:T(8,128)S(1)} %fusion.61), channel_id=1, source_target_pairs={{0,16},{8,24},{16,0},{24,8},{1,17},{9,25},{17,1},{25,9},{2,18},{10... | collective-permute-start | bytes 49160 | tf_op jit(solution)/shard_map/ppermute | solution.py:48
  220.6 24.6 %collective-permute-start.35 = (f32[4,32,32]{2,1,0:T(8,128)S(1)}, f32[4,32,32]{2,1,0:T(8,128)S(1)}, u32[]{:S(2)}, u32[]{:S(2)}) collective-permute-start(f32[4,32,32]{2,1,0:T(8,128)S(1)} %fusion.61), channel_id=1, source_target_pairs={{0,8},{8,0},{16,24},{24,16},{1,9},{9,1},{17,25},{25,17},{2,10},{10... | collective-permute-start | bytes 49160 | tf_op jit(solution)/shard_map/ppermute | solution.py:48
  254.7 13.3 %collective-permute-start.40 = (bf16[32,4608]{1,0:T(8,128)(2,1)S(1)}, bf16[32,4608]{1,0:T(8,128)(2,1)}, u32[]{:S(2)}, u32[]{:S(2)}) collective-permute-start(bf16[32,4608]{1,0:T(8,128)(2,1)S(1)} %get-tuple-element.34), channel_id=1, source_target_pairs={{0,24},{8,16},{16,8},{24,0},{1,25},{9,17},{17,9},{25,1},{2,26},{10... | collective-permute-start | bytes 884744 | tf_op jit(solution)/shard_map/ppermute | solution.py:48
  255.3 14.1 %collective-permute-start.39 = (bf16[32,4608]{1,0:T(8,128)(2,1)S(1)}, bf16[32,4608]{1,0:T(8,128)(2,1)}, u32[]{:S(2)}, u32[]{:S(2)}) collective-permute-start(bf16[32,4608]{1,0:T(8,128)(2,1)S(1)} %get-tuple-element.35), channel_id=1, source_target_pairs={{0,16},{8,24},{16,0},{24,8},{1,17},{9,25},{17,1},{25,9},{2,18},{10... | collective-permute-start | bytes 884744 | tf_op jit(solution)/shard_map/ppermute | solution.py:48
  284.2 30.4 %collective-permute-start.46 = (bf16[128,1024]{1,0:T(8,128)(2,1)S(1)}, bf16[128,1024]{1,0:T(8,128)(2,1)S(1)}, u32[]{:S(2)}, u32[]{:S(2)}) collective-permute-start(bf16[128,1024]{1,0:T(8,128)(2,1)S(1)} %pad_maximum_fusion.9), channel_id=1, source_target_pairs={{0,6},{1,7},{10,12},{11,13},{20,18},{21,19},{30,24},{31,25}} | collective-permute-start | bytes 786440 | tf_op jit(solution)/shard_map/ppermute | solution.py:182
  287.9 26.7 %collective-permute-start.45 = (bf16[128,1024]{1,0:T(8,128)(2,1)S(1)}, bf16[128,1024]{1,0:T(8,128)(2,1)S(1)}, u32[]{:S(2)}, u32[]{:S(2)}) collective-permute-start(bf16[128,1024]{1,0:T(8,128)(2,1)S(1)} %pad_maximum_fusion.9), channel_id=1, source_target_pairs={{0,4},{1,5},{10,14},{11,15},{20,16},{21,17},{30,26},{31,27}} | collective-permute-start | bytes 786440 | tf_op jit(solution)/shard_map/ppermute | solution.py:182
  289.2 25.4 %collective-permute-start.44 = (bf16[128,1024]{1,0:T(8,128)(2,1)S(1)}, bf16[128,1024]{1,0:T(8,128)(2,1)S(1)}, u32[]{:S(2)}, u32[]{:S(2)}) collective-permute-start(bf16[128,1024]{1,0:T(8,128)(2,1)S(1)} %pad_maximum_fusion.9), channel_id=1, source_target_pairs={{0,2},{1,3},{10,8},{11,9},{20,22},{21,23},{30,28},{31,29}} | collective-permute-start | bytes 786440 | tf_op jit(solution)/shard_map/ppermute | solution.py:182
  320.6 12.6 %collective-permute-start.48 = (bf16[896,128]{1,0:T(8,128)(2,1)S(1)}, bf16[896,128]{1,0:T(8,128)(2,1)S(1)}, u32[]{:S(2)}, u32[]{:S(2)}) collective-permute-start(bf16[896,128]{1,0:T(8,128)(2,1)S(1)} %get-tuple-element.38), channel_id=1, source_target_pairs={{0,2},{1,3},{2,0},{3,1},{4,6},{5,7},{6,4},{7,5},{8,10},{9,11},{10,... | collective-permute-start | bytes 688136 | tf_op jit(solution)/shard_map/ppermute | solution.py:48
  320.7 12.5 %collective-permute-start.50 = (bf16[896,128]{1,0:T(8,128)(2,1)S(1)}, bf16[896,128]{1,0:T(8,128)(2,1)S(1)}, u32[]{:S(2)}, u32[]{:S(2)}) collective-permute-start(bf16[896,128]{1,0:T(8,128)(2,1)S(1)} %get-tuple-element.39), channel_id=1, source_target_pairs={{0,6},{1,7},{2,4},{3,5},{4,2},{5,3},{6,0},{7,1},{8,14},{9,15},{10,... | collective-permute-start | bytes 688136 | tf_op jit(solution)/shard_map/ppermute | solution.py:48
  320.8 23.5 %collective-permute-start.49 = (bf16[896,128]{1,0:T(8,128)(2,1)S(1)}, bf16[896,128]{1,0:T(8,128)(2,1)S(1)}, u32[]{:S(2)}, u32[]{:S(2)}) collective-permute-start(bf16[896,128]{1,0:T(8,128)(2,1)S(1)} %get-tuple-element.40), channel_id=1, source_target_pairs={{0,4},{1,5},{2,6},{3,7},{4,0},{5,1},{6,2},{7,3},{8,12},{9,13},{10,... | collective-permute-start | bytes 688136 | tf_op jit(solution)/shard_map/ppermute | solution.py:48
  325.7 19.6 %collective-permute-start.55 = (bf16[128,1024]{1,0:T(8,128)(2,1)S(1)}, bf16[128,1024]{1,0:T(8,128)(2,1)S(1)}, u32[]{:S(2)}, u32[]{:S(2)}) collective-permute-start(bf16[128,1024]{1,0:T(8,128)(2,1)S(1)} %add_add_fusion), channel_id=1, source_target_pairs={{0,1},{1,0},{2,3},{3,2},{4,5},{5,4},{6,7},{7,6},{8,9},{9,8},{10,11... | collective-permute-start | bytes 786440 | tf_op jit(solution)/shard_map/ppermute | solution.py:48
  (62 other events, 463.3 us)
where the time goes:
time: 375 us; the launch traced here: 374 us
  waiting for transfers between devices  116 us (31%)
  Pallas kernels  94.1 us (25%)
  starting transfers between devices  74.2 us (20%)
  matrix products  40.4 us (11%)
  local copies, waits for them, and re-layouts  25.7 us (7%)
  other arithmetic  21.9 us (6%)
    ppermute x60, waiting for transfers between devices, xor_permute(): return lax.ppermute(x, axis, [(i, i ^ bits) for i in range(size)])  116 us
    ppermute x60, starting transfers between devices, xor_permute(): return lax.ppermute(x, axis, [(i, i ^ bits) for i in range(size)])  67.9 us
    pallas_call x1, Pallas kernels, moment_pass(): pl.pallas_call(functools.partial(moment_kernel, width), out_shape=[jax.Sh...  44.5 us
    dot_general x4, matrix products, rotate_in(): lax.dot_general(both, rows, (((0,), (0,)), ((), ())), preferred_element_t...  29.4 us
    pallas_call x1, Pallas kernels, right_pass(): pl.pallas_call(functools.partial(right_kernel, parts), out_shape=jax.Shap...  23.1 us
    pallas_call x1, Pallas kernels, cross_pass(): pl.pallas_call(cross_kernel, out_shape=jax.ShapeDtypeStruct((QUERIES * RA...  22.4 us
    select_n x16, other arithmetic, in_order(): parts = [jnp.where(on, parts[s ^ bit], parts[s]) for s in range(len(parts))]  9.37 us
  transfers between devices with their start and end apart: 63, of which 36 were waited for; matrix products, arithmetic and copies ran while one was open for 14% of the time, Pallas kernels for 24%

commit v1 on v0

--- a/solution.py
+++ b/solution.py
@@ -33,15 +33,15 @@
 
 
 def hold(x, *others):
-    others = [other[:16, :128] for other in others]
+    other = sum(other[:16, :128].astype(f32) for other in others)
     return pl.pallas_call(
         lambda *refs: None,
         out_shape=jax.ShapeDtypeStruct(x.shape, x.dtype),
-        in_specs=[pl.BlockSpec(memory_space=pl.ANY)] * (1 + len(others)),
+        in_specs=[pl.BlockSpec(memory_space=pl.ANY)] * 2,
         out_specs=pl.BlockSpec(memory_space=pl.ANY),
         input_output_aliases={0: 0},
         name="hold",
-    )(x, *others)
+    )(x, other)
 
 
 def xor_permute(x, axis, size, bits):
@@ -96,12 +96,14 @@
         kept = lax.dynamic_slice_in_dim(x, on * half, half, 0)
         given = lax.dynamic_slice_in_dim(x, (1 - on) * half, half, 0)
         x = kept + xor_permute(given.astype(f32 if n else bf16), "basis", size, bit).astype(f32)
+        if n == 0:
+            early = x
     x = x.astype(bf16)
     for bit in bits[::-1]:
         on = (me & bit) // bit
         late = x
         x = jnp.concatenate(in_order([x, xor_permute(x, "basis", size, bit)], on), axis=0)
-    return x, late
+    return x, early, late
 
 
 def reduce_rotated(x):
@@ -109,12 +111,12 @@
     while 1 << len(bits) < lax.axis_size("basis"):
         bits.append(1 << len(bits))
     half = x.shape[0] // 2
-    upper, _ = halve_basis(x[:half], bits)
-    lower, late = halve_basis(x[half:], bits[::-1])
-    return jnp.concatenate([upper, lower], axis=0), late
-
-
-def scatter_docs(x, dim, near, far):
+    upper, *upper_marks = halve_basis(x[:half], bits)
+    lower, *lower_marks = halve_basis(x[half:], bits[::-1])
+    return jnp.concatenate([upper, lower], axis=0), list(zip(upper_marks, lower_marks))
+
+
+def scatter_docs(x, dim, near, far, after=None):
     size = lax.axis_size("docs")
     me = lax.axis_index("docs")
     core, place = me % CORES, me // CORES
@@ -122,6 +124,8 @@
     kept = lax.dynamic_slice_in_dim(x, core * half, half, dim).astype(f32)
     given = lax.dynamic_slice_in_dim(x, (1 - core) * half, half, dim).astype(near)
     chip = kept + xor_permute(given, "docs", size, 1).astype(f32)
+    if after is not None:
+        chip = hold(chip, after)
     return scatter_direct(chip, "docs", size // CORES, place, CORES, dim, far).astype(bf16)
 
 
@@ -194,6 +198,8 @@
     rows, cols = values_ref.shape
     sides = [out_ref[:, q * LQ : (q + 1) * LQ] for q in range(QUERIES)]
 
+    sketch_ref[...] = jnp.zeros_like(sketch_ref)
+
     def step(c, carry):
         at = pl.ds(pl.multiple_of(c * width, width), width)
         weight = 1.0 / (values_ref[:, at].astype(f32) + damping)
@@ -201,17 +207,14 @@
             product = jnp.dot(
                 sides[q], in_ref[q * LQ : (q + 1) * LQ, at], preferred_element_type=f32
             )
-            moment_refs[q][:, at] = (product * weight).astype(bf16)
+            moment = (product * weight).astype(bf16)
+            moment_refs[q][:, at] = moment
+            sketch_ref[q * RANK : (q + 1) * RANK, :] += lax.dot_general(
+                test_ref[:, at], moment, (((1,), (1,)), ((), ())), preferred_element_type=f32
+            )
         return carry
 
     lax.fori_loop(0, cols // width, step, 0)
-    for q in range(QUERIES):
-        sketch_ref[q * RANK : (q + 1) * RANK, :] = lax.dot_general(
-            test_ref[...],
-            moment_refs[q][...],
-            (((1,), (1,)), ((), ())),
-            preferred_element_type=f32,
-        )
 
 
 def moment_pass(rot_out, rot_in, eigvals, test):
@@ -333,7 +336,7 @@
     )(*[eig_in] * parts, projected)
 
 
-def rotate_in(eig_in, in_factors, ready):
+def rotate_in(eig_in, in_factors):
     size = lax.axis_size("docs")
     places = size // CORES
     me = lax.axis_index("docs")
@@ -346,19 +349,16 @@
             low = s & -s
             chunks.append(xor_permute(chunks[s - low], "docs", size, CORES * low))
     for s, chunk in enumerate(chunks):
-        if s > 1:
+        if s & (s - 1):
             chunk = hold(chunk, totals[1])
         mate = xor_permute(chunk, "docs", size, 1)
-        if s == places - 1:
-            ready = hold(ready, totals[s - 1])
-            mate = hold(mate, ready)
         both = jnp.concatenate(in_order([chunk, mate], core), axis=0)
         rows = lax.dynamic_slice_in_dim(eig_in, (place ^ s) * depth, depth, 0)
         product = lax.dot_general(
             both, rows, (((0,), (0,)), ((), ())), preferred_element_type=f32
         )
         totals.append(totals[-1] + product if totals else product)
-    return totals[-1], ready
+    return totals[-1]
 
 
 def local(
@@ -378,13 +378,13 @@
     docs = lax.axis_size("docs")
 
     part_out = jnp.dot(eig_out, out_factors, preferred_element_type=f32)
-    mine_out = scatter_docs(part_out, 0, f32, bf16)
-    part_in, mine_out = rotate_in(eig_in, in_factors, mine_out)
-    rot_out = gather_docs(hold(mine_out, part_in), 0)
-    rot_in, late = reduce_rotated(part_in)
+    part_in = rotate_in(eig_in, in_factors)
+    rot_in, (early, late) = reduce_rotated(part_in)
+    rot_out = scatter_docs(part_out, 0, f32, bf16, after=part_in)
+    rot_out = gather_docs(hold(rot_out, *early), 0)
 
     moments, part = moment_pass(rot_out, rot_in, eigvals, jnp.transpose(test_matrix))
-    all_tokens = regroup_far(hold(regroup_near(activations), late))
+    all_tokens = regroup_far(hold(regroup_near(activations), late[1]))
     part = hold(part, *all_tokens[1:])
     sketch = gather_docs(scatter_docs(part, 1, f32, bf16), 1)
     split = sketch.reshape(QUERIES, RANK, sketch.shape[1])

time: 375 us -> 371 us (0.989)
  Pallas kernels: 94.1 us -> 104 us
  local copies, waits for them, and re-layouts: 25.7 us -> 16.9 us
  other arithmetic: 21.9 us -> 26.9 us
  waiting for transfers between devices: 116 us -> 112 us
    pallas_call x1, Pallas kernels: 44.5 us -> 54.8 us  [moment_pass(): pl.pallas_call(functools.partial(moment_kernel, width), out_shape=[jax.Sh...]
    slice x10 -> x3, local copies, waits for them, and re-layouts: 7.5 us -> 1.43 us  [the longest x2 1.19 us: hold(): other = sum((other[:16, :128].astype(f32) for other in others))]
    ppermute x60, waiting for transfers between devices: 116 us -> 112 us  [xor_permute(): return lax.ppermute(x, axis, [(i, i ^ bits) for i in range(size)])]
  transfers between devices with their start and end apart: 63 -> 63, of which waited for: 36 -> 34; matrix products, arithmetic and copies ran while one was open for 14% -> 12% of each run, Pallas kernels for 24% -> 27%
where the time goes in v1:
time: 371 us; the launch traced here: 370 us
  waiting for transfers between devices  112 us (30%)
  Pallas kernels  104 us (28%)
  starting transfers between devices  70.8 us (19%)
  matrix products  37.6 us (10%)
  other arithmetic  26.9 us (7%)
  local copies, waits for them, and re-layouts  16.9 us (5%)
    ppermute x60, waiting for transfers between devices, xor_permute(): return lax.ppermute(x, axis, [(i, i ^ bits) for i in range(size)])  112 us
    ppermute x60, starting transfers between devices, xor_permute(): return lax.ppermute(x, axis, [(i, i ^ bits) for i in range(size)])  64.5 us
    pallas_call x1, Pallas kernels, moment_pass(): pl.pallas_call(functools.partial(moment_kernel, width), out_shape=[jax.Sh...  54.8 us
    dot_general x4, matrix products, rotate_in(): lax.dot_general(both, rows, (((0,), (0,)), ((), ())), preferred_element_t...  26.6 us
    pallas_call x1, Pallas kernels, right_pass(): pl.pallas_call(functools.partial(right_kernel, parts), out_shape=jax.Shap...  23.1 us
    pallas_call x1, Pallas kernels, cross_pass(): pl.pallas_call(cross_kernel, out_shape=jax.ShapeDtypeStruct((QUERIES * RA...  22.4 us
    select_n x16, other arithmetic, in_order(): parts = [jnp.where(on, parts[s ^ bit], parts[s]) for s in range(len(parts))]  8.71 us
  transfers between devices with their start and end apart: 63, of which 34 were waited for; matrix products, arithmetic and copies ran while one was open for 12% of the time, Pallas kernels for 27%

profile of v1, /device:TPU:0, one launch (start us, length us, event | category | flops | bytes accessed | tf_op | source)
XLA Modules:
  0.0 369.7 jit_solution(1675533363520597805)
XLA Ops:
  1.2 3.7 collective-permute-start.4
  7.7 3.4 fusion.59
  12.7 13.4 %collective-permute-done.4 = bf16[896,256]{1,0:T(8,128)(2,1)} collective-permute-done((bf16[896,256]{1,0:T(8,128)(2,1)}, bf16[896,256]{1,0:T(8,128)(2,1)}, u32[]{:S(2)}, u32[]{:S(2)}) %collective-permute-start.4) | collective-permute-done | bytes 458784 | tf_op jit(solution)/shard_map/ppermute | solution.py:48
  28.6 6.6 %fusion.6 = f32[256,3584]{1,0:T(8,128)S(1)} fusion(bf16[7168,3584]{1,0:T(8,128)(2,1)} %refs_3_.1, s32[]{:T(128)S(6)} %select_n.456, bf16[896,256]{1,0:T(8,128)(2,1)S(1)} %get-tuple-element.50, bf16[896,256]{1,0:T(8,128)(2,1)S(1)} %get-tuple-element.49), kind=kOutput, calls=%fused_computation.6 | convolution fusion | flops 3290169344 | bytes 17432580 | tf_op jit(solution)/shard_map/dot_general | solution.py:357
  36.3 6.6 %fusion.8 = f32[256,3584]{1,0:T(8,128)S(1)} fusion(f32[256,3584]{1,0:T(8,128)S(1)} %fusion.6, bf16[7168,3584]{1,0:T(8,128)(2,1)} %refs_3_.1, s32[]{:T(128)S(6)} %select_n.459, bf16[896,256]{1,0:T(8,128)(2,1)S(1)} %get-tuple-element.48, bf16[896,256]{1,0:T(8,128)(2,1)S(1)} %get-tuple-element.47), kind=kOutput, calls=%fused_computation.8 | convolution fusion | flops 3291086848 | bytes 21102596 | tf_op jit(solution)/shard_map/dot_general | solution.py:357
  53.0 6.7 %fusion = f32[256,3584]{1,0:T(8,128)S(1)} fusion(bf16[7168,3584]{1,0:T(8,128)(2,1)} %refs_3_.1, s32[]{:T(128)S(6)} %select_n.465, bf16[896,256]{1,0:T(8,128)(2,1)S(1)} %get-tuple-element.46, bf16[896,256]{1,0:T(8,128)(2,1)S(1)} %get-tuple-element.45), kind=kOutput, calls=%fused_computation | convolution fusion | flops 3290169344 | bytes 17432580 | tf_op jit(solution)/shard_map/dot_general | solution.py:357
  59.8 6.6 %fusion.14 = f32[256,3584]{1,0:T(8,128)S(1)} fusion(f32[256,3584]{1,0:T(8,128)S(1)} %fusion, f32[256,3584]{1,0:T(8,128)S(1)} %copy-done.19, bf16[7168,3584]{1,0:T(8,128)(2,1)} %refs_3_.1, s32[]{:T(128)S(6)} %select_n.462, bf16[896,256]{1,0:T(8,128)(2,1)S(1)} %get-tuple-element.44, bf16[896,256]{1,0:T(8,128)(2,1)S(1)} %get-tuple-element.43), kind=kOutput, calls=%fused_computation.10 | convolution fusion | flops 3292004352 | bytes 24772612 | tf_op jit(solution)/shard_map/dot_general | solution.py:357
  78.1 5.6 %collective-permute-done.17 = bf16[256,256]{1,0:T(8,128)(2,1)S(1)} collective-permute-done((bf16[256,256]{1,0:T(8,128)(2,1)S(1)}, bf16[256,256]{1,0:T(8,128)(2,1)S(1)}, u32[]{:S(2)}, u32[]{:S(2)}) %collective-permute-start.17) | collective-permute-done | bytes 131104 | tf_op jit(solution)/shard_map/ppermute | solution.py:48
  83.7 4.1 %collective-permute-done.16 = bf16[256,256]{1,0:T(8,128)(2,1)S(1)} collective-permute-done((bf16[256,256]{1,0:T(8,128)(2,1)S(1)}, bf16[256,256]{1,0:T(8,128)(2,1)S(1)}, u32[]{:S(2)}, u32[]{:S(2)}) %collective-permute-start.16) | collective-permute-done | bytes 131104 | tf_op jit(solution)/shard_map/ppermute | solution.py:48
  98.7 5.3 %collective-permute-done.20 = bf16[256,256]{1,0:T(8,128)(2,1)S(1)} collective-permute-done((bf16[256,256]{1,0:T(8,128)(2,1)}, bf16[256,256]{1,0:T(8,128)(2,1)S(1)}, u32[]{:S(2)}, u32[]{:S(2)}) %collective-permute-start.20) | collective-permute-done | bytes 131104 | tf_op jit(solution)/shard_map/ppermute | solution.py:48
  127.5 54.8 %moment_pass.1 = (bf16[2048,3584]{1,0:T(8,128)(2,1)}, bf16[2048,3584]{1,0:T(8,128)(2,1)}, bf16[2048,3584]{1,0:T(8,128)(2,1)}, bf16[2048,3584]{1,0:T(8,128)(2,1)}, f32[128,2048]{1,0:T(8,128)}) custom-call(bf16[2048,256]{1,0:T(8,128)(2,1)} %pad_maximum_fusion.4.out_ref, bf16[256,3584]{1,0:T(8,128)(2,1)} %pad_maximum_fusion.2.in_ref, ...), custom_call_target="tpu_custom_call" | custom-call | flops 60129542144 | bytes 73400320 | tf_op jit(solution)/shard_map/moment_pass/pallas_call | solution.py:224
  193.1 4.2 %collective-permute-done.30 = bf16[128,256]{1,0:T(8,128)(2,1)S(1)} collective-permute-done((bf16[128,256]{1,0:T(8,128)(2,1)S(1)}, bf16[128,256]{1,0:T(8,128)(2,1)S(1)}, u32[]{:S(2)}, u32[]{:S(2)}) %collective-permute-start.30) | collective-permute-done | bytes 65568 | tf_op jit(solution)/shard_map/ppermute | solution.py:48
  216.9 22.4 %cross_pass.1 = f32[128,3584]{1,0:T(8,128)} custom-call(bf16[128,2048]{1,0:T(8,128)(2,1)} %copy-done.3, bf16[2048,3584]{1,0:T(8,128)(2,1)} %get-tuple-element.8.refs_0_, bf16[2048,3584]{1,0:T(8,128)(2,1)} %get-tuple-element.9.refs_1_, bf16[2048,3584]{1,0:T(8,128)(2,1)} %get-tuple-element.10.refs_2_, bf16[2048,3584]{1,0:T(8,128)(2,1)} %get-tuple-element.11.refs_3_), custom_call_target="tpu_custom_call" | custom-call | flops 15032385536 | bytes 58720256 | tf_op jit(solution)/shard_map/cross_pass/pallas_call | solution.py:259
  241.6 4.1 %inverse_factor.1 = f32[4,32,32]{2,1,0:T(8,128)} custom-call(f32[4,32,32]{2,1,0:T(8,128)} %add_add_fusion.2.gram_ref), custom_call_target="tpu_custom_call" | custom-call | tf_op jit(solution)/shard_map/inverse_factor/pallas_call | solution.py:292
  252.4 6.6 %collective-permute-done.38 = bf16[32,4608]{1,0:T(8,128)(2,1)} collective-permute-done((bf16[32,4608]{1,0:T(8,128)(2,1)S(1)}, bf16[32,4608]{1,0:T(8,128)(2,1)}, u32[]{:S(2)}, u32[]{:S(2)}) %collective-permute-start.38) | collective-permute-done | bytes 294944 | tf_op jit(solution)/shard_map/ppermute | solution.py:48
  259.0 5.0 %collective-permute-done.40 = bf16[32,4608]{1,0:T(8,128)(2,1)} collective-permute-done((bf16[32,4608]{1,0:T(8,128)(2,1)S(1)}, bf16[32,4608]{1,0:T(8,128)(2,1)}, u32[]{:S(2)}, u32[]{:S(2)}) %collective-permute-start.40) | collective-permute-done | bytes 294944 | tf_op jit(solution)/shard_map/ppermute | solution.py:48
  270.2 5.5 %collective-permute-done.43 = bf16[32,4608]{1,0:T(8,128)(2,1)S(1)} collective-permute-done((bf16[32,4608]{1,0:T(8,128)(2,1)S(1)}, bf16[32,4608]{1,0:T(8,128)(2,1)S(1)}, u32[]{:S(2)}, u32[]{:S(2)}) %collective-permute-start.43) | collective-permute-done | bytes 294944 | tf_op jit(solution)/shard_map/ppermute | solution.py:48
  275.7 4.4 %collective-permute-done.42 = bf16[32,4608]{1,0:T(8,128)(2,1)S(1)} collective-permute-done((bf16[32,4608]{1,0:T(8,128)(2,1)S(1)}, bf16[32,4608]{1,0:T(8,128)(2,1)S(1)}, u32[]{:S(2)}, u32[]{:S(2)}) %collective-permute-start.42) | collective-permute-done | bytes 294944 | tf_op jit(solution)/shard_map/ppermute | solution.py:48
  280.3 3.7 collective-permute-start.46
  287.7 23.1 %right_pass.1.refs_0_ = bf16[7168,128]{1,0:T(8,128)(2,1)} custom-call(bf16[7168,3584]{1,0:T(8,128)(2,1)} %refs_3_.1, bf16[7168,3584]{1,0:T(8,128)(2,1)} %refs_3_.1, bf16[7168,3584]{1,0:T(8,128)(2,1)} %refs_3_.1, bf16[7168,3584]{1,0:T(8,128)(2,1)} %refs_3_.1, bf16[128,3584]{1,0:T(8,128)(2,1)} %slice.70.refs_4_), custom_call_target="tpu_custom_call" | custom-call | flops 13153337344 | bytes 51380224 | tf_op jit(solution)/shard_map/right_pass/pallas_call | solution.py:319
  316.9 3.4 collective-permute-start.49
  321.9 7.5 %collective-permute-done.48 = bf16[896,128]{1,0:T(8,128)(2,1)S(1)} collective-permute-done((bf16[896,128]{1,0:T(8,128)(2,1)S(1)}, bf16[896,128]{1,0:T(8,128)(2,1)S(1)}, u32[]{:S(2)}, u32[]{:S(2)}) %collective-permute-start.48) | collective-permute-done | bytes 229408 | tf_op jit(solution)/shard_map/ppermute | solution.py:48
  329.4 11.0 %collective-permute-done.49 = bf16[896,128]{1,0:T(8,128)(2,1)S(1)} collective-permute-done((bf16[896,128]{1,0:T(8,128)(2,1)S(1)}, bf16[896,128]{1,0:T(8,128)(2,1)S(1)}, u32[]{:S(2)}, u32[]{:S(2)}) %collective-permute-start.49) | collective-permute-done | bytes 229408 | tf_op jit(solution)/shard_map/ppermute | solution.py:48
  356.4 3.5 collective-permute-done.57
  (243 shorter events, 147.0 us)
Async XLA Ops:
  0.6 26.2 %collective-permute-start.1 = (bf16[896,256]{1,0:T(8,128)(2,1)}, bf16[896,256]{1,0:T(8,128)(2,1)}, u32[]{:S(2)}, u32[]{:S(2)}) collective-permute-start(bf16[896,256]{1,0:T(8,128)(2,1)} %param.13), channel_id=1, source_target_pairs={{0,1},{1,0},{2,3},{3,2},{4,5},{5,4},{6,7},{7,6},{8,9},{9,8},{10,11... | collective-permute-start | bytes 1376264 | tf_op jit(solution)/shard_map/ppermute | solution.py:48
  1.2 25.0 %collective-permute-start.4 = (bf16[896,256]{1,0:T(8,128)(2,1)}, bf16[896,256]{1,0:T(8,128)(2,1)}, u32[]{:S(2)}, u32[]{:S(2)}) collective-permute-start(bf16[896,256]{1,0:T(8,128)(2,1)} %param.13), channel_id=1, source_target_pairs={{0,4},{1,5},{2,6},{3,7},{4,0},{5,1},{6,2},{7,3},{8,12},{9,13},{10,... | collective-permute-start | bytes 1376264 | tf_op jit(solution)/shard_map/ppermute | solution.py:48
  4.8 22.0 %collective-permute-start.2 = (bf16[896,256]{1,0:T(8,128)(2,1)}, bf16[896,256]{1,0:T(8,128)(2,1)}, u32[]{:S(2)}, u32[]{:S(2)}) collective-permute-start(bf16[896,256]{1,0:T(8,128)(2,1)} %param.13), channel_id=1, source_target_pairs={{0,2},{1,3},{2,0},{3,1},{4,6},{5,7},{6,4},{7,5},{8,10},{9,11},{10,... | collective-permute-start | bytes 1376264 | tf_op jit(solution)/shard_map/ppermute | solution.py:48
  7.6 38.5 %collective-permute-start = (bf16[128,3584]{1,0:T(8,128)(2,1)S(1)}, bf16[128,3584]{1,0:T(8,128)(2,1)}, u32[]{:S(2)}, u32[]{:S(2)}) collective-permute-start(bf16[128,3584]{1,0:T(8,128)(2,1)S(1)} %constant_dynamic-slice_fusion.25), channel_id=1, source_target_pairs={{0,1},{1,0},{2,3},{3,2},{4,5},{5,4},{6,7},{7,6},{8,9},{9,8},{10,11... | collective-permute-start | bytes 2752520 | tf_op jit(solution)/shard_map/ppermute | solution.py:48
  12.3 38.3 %collective-permute-start.14 = (f32[1024,256]{1,0:T(8,128)}, f32[1024,256]{1,0:T(8,128)}, u32[]{:S(2)}, u32[]{:S(2)}) collective-permute-start(f32[1024,256]{1,0:T(8,128)} %constant_dynamic-slice_fusion.20), channel_id=1, source_target_pairs={{0,1},{1,0},{2,3},{3,2},{4,5},{5,4},{6,7},{7,6},{8,9},{9,8},{10,11... | collective-permute-start | bytes 3145736 | tf_op jit(solution)/shard_map/ppermute | solution.py:48
  26.2 19.1 %collective-permute-start.6 = (bf16[896,256]{1,0:T(8,128)(2,1)}, bf16[896,256]{1,0:T(8,128)(2,1)S(1)}, u32[]{:S(2)}, u32[]{:S(2)}) collective-permute-start(bf16[896,256]{1,0:T(8,128)(2,1)} %collective-permute-done.4), channel_id=1, source_target_pairs={{0,2},{1,3},{2,0},{3,1},{4,6},{5,7},{6,4},{7,5},{8,10},{9,11},{10,... | collective-permute-start | bytes 1376264 | tf_op jit(solution)/shard_map/ppermute | solution.py:48
  26.8 22.4 %collective-permute-start.5 = (bf16[896,256]{1,0:T(8,128)(2,1)}, bf16[896,256]{1,0:T(8,128)(2,1)}, u32[]{:S(2)}, u32[]{:S(2)}) collective-permute-start(bf16[896,256]{1,0:T(8,128)(2,1)} %collective-permute-done.4), channel_id=1, source_target_pairs={{0,1},{1,0},{2,3},{3,2},{4,5},{5,4},{6,7},{7,6},{8,9},{9,8},{10,11... | collective-permute-start | bytes 1376264 | tf_op jit(solution)/shard_map/ppermute | solution.py:48
  68.5 21.0 %collective-permute-start.8 = (bf16[64,3584]{1,0:T(8,128)(2,1)S(1)}, bf16[64,3584]{1,0:T(8,128)(2,1)S(1)}, u32[]{:S(2)}, u32[]{:S(2)}) collective-permute-start(bf16[64,3584]{1,0:T(8,128)(2,1)S(1)} %dynamic-slice_convert_fusion.1), channel_id=1, source_target_pairs={{0,16},{8,24},{16,0},{24,8},{1,17},{9,25},{17,1},{25,9},{2,18},{10... | collective-permute-start | bytes 1376264 | tf_op jit(solution)/shard_map/ppermute | solution.py:48
  76.5 13.1 %collective-permute-start.18 = (bf16[64,3584]{1,0:T(8,128)(2,1)S(1)}, bf16[64,3584]{1,0:T(8,128)(2,1)S(1)}, u32[]{:S(2)}, u32[]{:S(2)}) collective-permute-start(bf16[64,3584]{1,0:T(8,128)(2,1)S(1)} %dynamic-slice_convert_fusion), channel_id=1, source_target_pairs={{0,8},{8,0},{16,24},{24,16},{1,9},{9,1},{17,25},{25,17},{2,10},{10... | collective-permute-start | bytes 1376264 | tf_op jit(solution)/shard_map/ppermute | solution.py:48
  91.1 12.9 %collective-permute-start.20 = (bf16[256,256]{1,0:T(8,128)(2,1)}, bf16[256,256]{1,0:T(8,128)(2,1)S(1)}, u32[]{:S(2)}, u32[]{:S(2)}) collective-permute-start(bf16[256,256]{1,0:T(8,128)(2,1)} %hold.9), channel_id=1, source_target_pairs={{0,4},{1,5},{2,6},{3,7},{4,0},{5,1},{6,2},{7,3},{8,12},{9,13},{10,... | collective-permute-start | bytes 393224 | tf_op jit(solution)/shard_map/ppermute | solution.py:48
  119.5 62.8 %collective-permute-start.13 = (bf16[256,896]{1,0:T(8,128)(2,1)S(1)}, bf16[256,896]{1,0:T(8,128)(2,1)S(1)}, u32[]{:S(2)}, u32[]{:S(2)}) collective-permute-start(bf16[256,896]{1,0:T(8,128)(2,1)S(1)} %get-tuple-element.24), channel_id=1, source_target_pairs={{0,2},{1,3},{2,0},{3,1},{4,6},{5,7},{6,4},{7,5},{8,10},{9,11},{10,... | collective-permute-start | bytes 1376264 | tf_op jit(solution)/shard_map/ppermute | solution.py:48
  119.6 62.7 %collective-permute-start.12 = (bf16[256,896]{1,0:T(8,128)(2,1)S(1)}, bf16[256,896]{1,0:T(8,128)(2,1)S(1)}, u32[]{:S(2)}, u32[]{:S(2)}) collective-permute-start(bf16[256,896]{1,0:T(8,128)(2,1)S(1)} %get-tuple-element.25), channel_id=1, source_target_pairs={{0,4},{1,5},{2,6},{3,7},{4,0},{5,1},{6,2},{7,3},{8,12},{9,13},{10,... | collective-permute-start | bytes 1376264 | tf_op jit(solution)/shard_map/ppermute | solution.py:48
  122.3 60.0 %collective-permute-start.11 = (bf16[256,896]{1,0:T(8,128)(2,1)S(1)}, bf16[256,896]{1,0:T(8,128)(2,1)S(1)}, u32[]{:S(2)}, u32[]{:S(2)}) collective-permute-start(bf16[256,896]{1,0:T(8,128)(2,1)S(1)} %get-tuple-element.26), channel_id=1, source_target_pairs={{0,6},{1,7},{2,4},{3,5},{4,2},{5,3},{6,0},{7,1},{8,14},{9,15},{10,... | collective-permute-start | bytes 1376264 | tf_op jit(solution)/shard_map/ppermute | solution.py:48
  213.4 27.6 %collective-permute-start.37 = (f32[4,32,32]{2,1,0:T(8,128)S(1)}, f32[4,32,32]{2,1,0:T(8,128)S(1)}, u32[]{:S(2)}, u32[]{:S(2)}) collective-permute-start(f32[4,32,32]{2,1,0:T(8,128)S(1)} %fusion.60), channel_id=1, source_target_pairs={{0,24},{8,16},{16,8},{24,0},{1,25},{9,17},{17,9},{25,1},{2,26},{10... | collective-permute-start | bytes 49160 | tf_op jit(solution)/shard_map/ppermute | solution.py:48
  215.2 25.7 %collective-permute-start.36 = (f32[4,32,32]{2,1,0:T(8,128)S(1)}, f32[4,32,32]{2,1,0:T(8,128)S(1)}, u32[]{:S(2)}, u32[]{:S(2)}) collective-permute-start(f32[4,32,32]{2,1,0:T(8,128)S(1)} %fusion.60), channel_id=1, source_target_pairs={{0,16},{8,24},{16,0},{24,8},{1,17},{9,25},{17,1},{25,9},{2,18},{10... | collective-permute-start | bytes 49160 | tf_op jit(solution)/shard_map/ppermute | solution.py:48
  215.7 25.2 %collective-permute-start.35 = (f32[4,32,32]{2,1,0:T(8,128)S(1)}, f32[4,32,32]{2,1,0:T(8,128)S(1)}, u32[]{:S(2)}, u32[]{:S(2)}) collective-permute-start(f32[4,32,32]{2,1,0:T(8,128)S(1)} %fusion.60), channel_id=1, source_target_pairs={{0,8},{8,0},{16,24},{24,16},{1,9},{9,1},{17,25},{25,17},{2,10},{10... | collective-permute-start | bytes 49160 | tf_op jit(solution)/shard_map/ppermute | solution.py:48
  249.8 14.2 %collective-permute-start.40 = (bf16[32,4608]{1,0:T(8,128)(2,1)S(1)}, bf16[32,4608]{1,0:T(8,128)(2,1)}, u32[]{:S(2)}, u32[]{:S(2)}) collective-permute-start(bf16[32,4608]{1,0:T(8,128)(2,1)S(1)} %get-tuple-element.32), channel_id=1, source_target_pairs={{0,24},{8,16},{16,8},{24,0},{1,25},{9,17},{17,9},{25,1},{2,26},{10... | collective-permute-start | bytes 884744 | tf_op jit(solution)/shard_map/ppermute | solution.py:48
  251.3 14.1 %collective-permute-start.39 = (bf16[32,4608]{1,0:T(8,128)(2,1)S(1)}, bf16[32,4608]{1,0:T(8,128)(2,1)}, u32[]{:S(2)}, u32[]{:S(2)}) collective-permute-start(bf16[32,4608]{1,0:T(8,128)(2,1)S(1)} %get-tuple-element.33), channel_id=1, source_target_pairs={{0,16},{8,24},{16,0},{24,8},{1,17},{9,25},{17,1},{25,9},{2,18},{10... | collective-permute-start | bytes 884744 | tf_op jit(solution)/shard_map/ppermute | solution.py:48
  280.3 30.4 %collective-permute-start.46 = (bf16[128,1024]{1,0:T(8,128)(2,1)S(1)}, bf16[128,1024]{1,0:T(8,128)(2,1)S(1)}, u32[]{:S(2)}, u32[]{:S(2)}) collective-permute-start(bf16[128,1024]{1,0:T(8,128)(2,1)S(1)} %pad_maximum_fusion.9), channel_id=1, source_target_pairs={{0,6},{1,7},{10,12},{11,13},{20,18},{21,19},{30,24},{31,25}} | collective-permute-start | bytes 786440 | tf_op jit(solution)/shard_map/ppermute | solution.py:186
  284.0 26.7 %collective-permute-start.45 = (bf16[128,1024]{1,0:T(8,128)(2,1)S(1)}, bf16[128,1024]{1,0:T(8,128)(2,1)S(1)}, u32[]{:S(2)}, u32[]{:S(2)}) collective-permute-start(bf16[128,1024]{1,0:T(8,128)(2,1)S(1)} %pad_maximum_fusion.9), channel_id=1, source_target_pairs={{0,4},{1,5},{10,14},{11,15},{20,16},{21,17},{30,26},{31,27}} | collective-permute-start | bytes 786440 | tf_op jit(solution)/shard_map/ppermute | solution.py:186
  285.4 25.4 %collective-permute-start.44 = (bf16[128,1024]{1,0:T(8,128)(2,1)S(1)}, bf16[128,1024]{1,0:T(8,128)(2,1)S(1)}, u32[]{:S(2)}, u32[]{:S(2)}) collective-permute-start(bf16[128,1024]{1,0:T(8,128)(2,1)S(1)} %pad_maximum_fusion.9), channel_id=1, source_target_pairs={{0,2},{1,3},{10,8},{11,9},{20,22},{21,23},{30,28},{31,29}} | collective-permute-start | bytes 786440 | tf_op jit(solution)/shard_map/ppermute | solution.py:186
  316.7 12.6 %collective-permute-start.48 = (bf16[896,128]{1,0:T(8,128)(2,1)S(1)}, bf16[896,128]{1,0:T(8,128)(2,1)S(1)}, u32[]{:S(2)}, u32[]{:S(2)}) collective-permute-start(bf16[896,128]{1,0:T(8,128)(2,1)S(1)} %get-tuple-element.36), channel_id=1, source_target_pairs={{0,2},{1,3},{2,0},{3,1},{4,6},{5,7},{6,4},{7,5},{8,10},{9,11},{10,... | collective-permute-start | bytes 688136 | tf_op jit(solution)/shard_map/ppermute | solution.py:48
  316.9 23.5 %collective-permute-start.49 = (bf16[896,128]{1,0:T(8,128)(2,1)S(1)}, bf16[896,128]{1,0:T(8,128)(2,1)S(1)}, u32[]{:S(2)}, u32[]{:S(2)}) collective-permute-start(bf16[896,128]{1,0:T(8,128)(2,1)S(1)} %get-tuple-element.38), channel_id=1, source_target_pairs={{0,4},{1,5},{2,6},{3,7},{4,0},{5,1},{6,2},{7,3},{8,12},{9,13},{10,... | collective-permute-start | bytes 688136 | tf_op jit(solution)/shard_map/ppermute | solution.py:48
  321.8 19.6 %collective-permute-start.55 = (bf16[128,1024]{1,0:T(8,128)(2,1)S(1)}, bf16[128,1024]{1,0:T(8,128)(2,1)S(1)}, u32[]{:S(2)}, u32[]{:S(2)}) collective-permute-start(bf16[128,1024]{1,0:T(8,128)(2,1)S(1)} %add_add_fusion), channel_id=1, source_target_pairs={{0,1},{1,0},{2,3},{3,2},{4,5},{5,4},{6,7},{7,6},{8,9},{9,8},{10,11... | collective-permute-start | bytes 786440 | tf_op jit(solution)/shard_map/ppermute | solution.py:48
  (60 other events, 425.5 us)

commit v2 on v1

--- a/solution.py
+++ b/solution.py
@@ -198,8 +198,6 @@
     rows, cols = values_ref.shape
     sides = [out_ref[:, q * LQ : (q + 1) * LQ] for q in range(QUERIES)]
 
-    sketch_ref[...] = jnp.zeros_like(sketch_ref)
-
     def step(c, carry):
         at = pl.ds(pl.multiple_of(c * width, width), width)
         weight = 1.0 / (values_ref[:, at].astype(f32) + damping)
@@ -207,20 +205,23 @@
             product = jnp.dot(
                 sides[q], in_ref[q * LQ : (q + 1) * LQ, at], preferred_element_type=f32
             )
-            moment = (product * weight).astype(bf16)
-            moment_refs[q][:, at] = moment
-            sketch_ref[q * RANK : (q + 1) * RANK, :] += lax.dot_general(
-                test_ref[:, at], moment, (((1,), (1,)), ((), ())), preferred_element_type=f32
-            )
+            moment_refs[q][:, at] = (product * weight).astype(bf16)
         return carry
 
     lax.fori_loop(0, cols // width, step, 0)
+    for q in range(QUERIES):
+        sketch_ref[q * RANK : (q + 1) * RANK, :] = lax.dot_general(
+            test_ref[...],
+            moment_refs[q][...],
+            (((1,), (1,)), ((), ())),
+            preferred_element_type=f32,
+        )
 
 
 def moment_pass(rot_out, rot_in, eigvals, test):
     rows, cols = eigvals.shape
     height = tile(rows, 256, 128)
-    width = tile(cols, 512, 128)
+    width = tile(cols, 1792, 128)
     *moments, sketch = pl.pallas_call(
         functools.partial(moment_kernel, width),
         out_shape=[jax.ShapeDtypeStruct((rows, cols), bf16)] * QUERIES
@@ -345,12 +346,14 @@
     depth = CORES * in_factors.shape[0]
     totals = []
     for s in range(places):
-        if s > 0:
-            low = s & -s
+        low = s & -s
+        if s == low and s > 0:
+            chunks.append(xor_permute(in_factors, "docs", size, CORES * s))
+        elif s > 0:
             chunks.append(xor_permute(chunks[s - low], "docs", size, CORES * low))
-    for s, chunk in enumerate(chunks):
-        if s & (s - 1):
-            chunk = hold(chunk, totals[1])
+        chunk = chunks[s]
+        if s > 1:
+            chunk = chunks[s] = hold(chunk, totals[0 if s == low else 1])
         mate = xor_permute(chunk, "docs", size, 1)
         both = jnp.concatenate(in_order([chunk, mate], core), axis=0)
         rows = lax.dynamic_slice_in_dim(eig_in, (place ^ s) * depth, depth, 0)

time: 371 us -> 360 us (0.970)
  Pallas kernels: 104 us -> 89.1 us
  local copies, waits for them, and re-layouts: 16.9 us -> 21.1 us
    pallas_call x1, Pallas kernels: 54.8 us -> 39.5 us  [moment_pass(): pl.pallas_call(functools.partial(moment_kernel, width), out_shape=[jax.Sh...]
    unnamed x42 -> x50, local copies, waits for them, and re-layouts: 5.62 us -> 8.21 us
  transfers between devices with their start and end apart: 63 -> 63, of which waited for: 34 -> 34; matrix products, arithmetic and copies ran while one was open for 12% -> 14% of each run, Pallas kernels for 27% -> 24%
where the time goes in v2:
time: 360 us
  waiting for transfers between devices  111 us (31%)
  Pallas kernels  89.1 us (25%)
  starting transfers between devices  70 us (19%)
  matrix products  40.4 us (11%)
  other arithmetic  26.6 us (7%)
  local copies, waits for them, and re-layouts  21.1 us (6%)
    ppermute x60, waiting for transfers between devices, xor_permute(): return lax.ppermute(x, axis, [(i, i ^ bits) for i in range(size)])  111 us
    ppermute x60, starting transfers between devices, xor_permute(): return lax.ppermute(x, axis, [(i, i ^ bits) for i in range(size)])  63.5 us
    pallas_call x1, Pallas kernels, moment_pass(): pl.pallas_call(functools.partial(moment_kernel, width), out_shape=[jax.Sh...  39.5 us
    dot_general x4, matrix products, rotate_in(): lax.dot_general(both, rows, (((0,), (0,)), ((), ())), preferred_element_t...  29.5 us
    pallas_call x1, Pallas kernels, right_pass(): pl.pallas_call(functools.partial(right_kernel, parts), out_shape=jax.Shap...  23.1 us
    pallas_call x1, Pallas kernels, cross_pass(): pl.pallas_call(cross_kernel, out_shape=jax.ShapeDtypeStruct((QUERIES * RA...  22.5 us
    select_n x16, other arithmetic, in_order(): parts = [jnp.where(on, parts[s ^ bit], parts[s]) for s in range(len(parts))]  8.43 us
    unnamed x50, local copies, waits for them, and re-layouts  8.21 us
  transfers between devices with their start and end apart: 63, of which 34 were waited for; matrix products, arithmetic and copies ran while one was open for 14% of the time, Pallas kernels for 24%

profile of v2, /device:TPU:0, one launch (start us, length us, event | category | flops | bytes accessed | tf_op | source)
XLA Modules:
  0.0 359.5 jit_solution(5773882504880519021)
XLA Ops:
  1.2 3.7 %collective-permute-start.4 = (bf16[896,256]{1,0:T(8,128)(2,1)}, bf16[896,256]{1,0:T(8,128)(2,1)S(1)}, u32[]{:S(2)}, u32[]{:S(2)}) collective-permute-start(bf16[896,256]{1,0:T(8,128)(2,1)} %param.13), channel_id=1, source_target_pairs={{0,4},{1,5},{2,6},{3,7},{4,0},{5,1},{6,2},{7,3},{8,12},{9,13},{10,... | collective-permute-start | bytes 1376264 | tf_op jit(solution)/shard_map/ppermute | solution.py:48
  8.6 3.4 fusion.59
  13.6 12.6 %collective-permute-done.2 = bf16[896,256]{1,0:T(8,128)(2,1)S(1)} collective-permute-done((bf16[896,256]{1,0:T(8,128)(2,1)}, bf16[896,256]{1,0:T(8,128)(2,1)S(1)}, u32[]{:S(2)}, u32[]{:S(2)}) %collective-permute-start.2) | collective-permute-done | bytes 458784 | tf_op jit(solution)/shard_map/ppermute | solution.py:48
  27.4 6.6 %fusion.6 = f32[256,3584]{1,0:T(8,128)S(1)} fusion(bf16[7168,3584]{1,0:T(8,128)(2,1)} %refs_3_.1, s32[]{:T(128)S(6)} %select_n.456, bf16[896,256]{1,0:T(8,128)(2,1)S(1)} %get-tuple-element.50, bf16[896,256]{1,0:T(8,128)(2,1)S(1)} %get-tuple-element.49), kind=kOutput, calls=%fused_computation.6 | convolution fusion | flops 3290169344 | bytes 17432580 | tf_op jit(solution)/shard_map/dot_general | solution.py:360
  40.0 9.3 %fusion.8 = f32[256,3584]{1,0:T(8,128)S(1)} fusion(f32[256,3584]{1,0:T(8,128)} %copy-done.23, bf16[7168,3584]{1,0:T(8,128)(2,1)} %refs_3_.1, s32[]{:T(128)S(6)} %select_n.459, bf16[896,256]{1,0:T(8,128)(2,1)S(1)} %get-tuple-element.48, bf16[896,256]{1,0:T(8,128)(2,1)S(1)} %get-tuple-element.47), kind=kOutput, calls=%fused_computation.8 | convolution fusion | flops 3291086848 | bytes 21102596 | tf_op jit(solution)/shard_map/dot_general | solution.py:360
  59.5 6.7 %fusion = f32[256,3584]{1,0:T(8,128)S(1)} fusion(bf16[7168,3584]{1,0:T(8,128)(2,1)} %refs_3_.1, s32[]{:T(128)S(6)} %select_n.465, bf16[896,256]{1,0:T(8,128)(2,1)S(1)} %get-tuple-element.46, bf16[896,256]{1,0:T(8,128)(2,1)S(1)} %get-tuple-element.45), kind=kOutput, calls=%fused_computation | convolution fusion | flops 3290169344 | bytes 17432580 | tf_op jit(solution)/shard_map/dot_general | solution.py:360
  66.3 6.8 %fusion.14 = f32[256,3584]{1,0:T(8,128)S(1)} fusion(f32[256,3584]{1,0:T(8,128)S(1)} %fusion, f32[256,3584]{1,0:T(8,128)S(1)} %copy-done.22, bf16[7168,3584]{1,0:T(8,128)(2,1)} %refs_3_.1, s32[]{:T(128)S(6)} %select_n.462, bf16[896,256]{1,0:T(8,128)(2,1)S(1)} %get-tuple-element.44, bf16[896,256]{1,0:T(8,128)(2,1)S(1)} %get-tuple-element.43), kind=kOutput, calls=%fused_computation.10 | convolution fusion | flops 3292004352 | bytes 24772612 | tf_op jit(solution)/shard_map/dot_general | solution.py:360
  87.2 6.1 %collective-permute-done.16 = bf16[256,256]{1,0:T(8,128)(2,1)S(1)} collective-permute-done((bf16[256,256]{1,0:T(8,128)(2,1)S(1)}, bf16[256,256]{1,0:T(8,128)(2,1)S(1)}, u32[]{:S(2)}, u32[]{:S(2)}) %collective-permute-start.16) | collective-permute-done | bytes 131104 | tf_op jit(solution)/shard_map/ppermute | solution.py:48
  104.2 4.9 %collective-permute-done.20 = bf16[256,256]{1,0:T(8,128)(2,1)S(1)} collective-permute-done((bf16[256,256]{1,0:T(8,128)(2,1)}, bf16[256,256]{1,0:T(8,128)(2,1)S(1)}, u32[]{:S(2)}, u32[]{:S(2)}) %collective-permute-start.20) | collective-permute-done | bytes 131104 | tf_op jit(solution)/shard_map/ppermute | solution.py:48
  132.5 39.5 %moment_pass.1 = (bf16[2048,3584]{1,0:T(8,128)(2,1)}, bf16[2048,3584]{1,0:T(8,128)(2,1)}, bf16[2048,3584]{1,0:T(8,128)(2,1)}, bf16[2048,3584]{1,0:T(8,128)(2,1)}, f32[128,2048]{1,0:T(8,128)}) custom-call(bf16[2048,256]{1,0:T(8,128)(2,1)} %pad_maximum_fusion.4.out_ref, bf16[256,3584]{1,0:T(8,128)(2,1)} %pad_maximum_fusion.2.in_ref, ...), custom_call_target="tpu_custom_call" | custom-call | flops 60129542144 | bytes 73400320 | tf_op jit(solution)/shard_map/moment_pass/pallas_call | solution.py:225
  182.8 4.1 %collective-permute-done.30 = bf16[128,256]{1,0:T(8,128)(2,1)S(1)} collective-permute-done((bf16[128,256]{1,0:T(8,128)(2,1)S(1)}, bf16[128,256]{1,0:T(8,128)(2,1)S(1)}, u32[]{:S(2)}, u32[]{:S(2)}) %collective-permute-start.30) | collective-permute-done | bytes 65568 | tf_op jit(solution)/shard_map/ppermute | solution.py:48
  194.1 3.4 collective-permute-done.32
  206.3 22.5 %cross_pass.1 = f32[128,3584]{1,0:T(8,128)} custom-call(bf16[128,2048]{1,0:T(8,128)(2,1)} %copy-done.3, bf16[2048,3584]{1,0:T(8,128)(2,1)} %get-tuple-element.8.refs_0_, bf16[2048,3584]{1,0:T(8,128)(2,1)} %get-tuple-element.9.refs_1_, bf16[2048,3584]{1,0:T(8,128)(2,1)} %get-tuple-element.10.refs_2_, bf16[2048,3584]{1,0:T(8,128)(2,1)} %get-tuple-element.11.refs_3_), custom_call_target="tpu_custom_call" | custom-call | flops 15032385536 | bytes 58720256 | tf_op jit(solution)/shard_map/cross_pass/pallas_call | solution.py:260
  231.1 4.1 %inverse_factor.1 = f32[4,32,32]{2,1,0:T(8,128)} custom-call(f32[4,32,32]{2,1,0:T(8,128)} %add_add_fusion.2.gram_ref), custom_call_target="tpu_custom_call" | custom-call | tf_op jit(solution)/shard_map/inverse_factor/pallas_call | solution.py:293
  242.0 6.6 %collective-permute-done.38 = bf16[32,4608]{1,0:T(8,128)(2,1)} collective-permute-done((bf16[32,4608]{1,0:T(8,128)(2,1)S(1)}, bf16[32,4608]{1,0:T(8,128)(2,1)}, u32[]{:S(2)}, u32[]{:S(2)}) %collective-permute-start.38) | collective-permute-done | bytes 294944 | tf_op jit(solution)/shard_map/ppermute | solution.py:48
  248.5 5.0 %collective-permute-done.40 = bf16[32,4608]{1,0:T(8,128)(2,1)} collective-permute-done((bf16[32,4608]{1,0:T(8,128)(2,1)S(1)}, bf16[32,4608]{1,0:T(8,128)(2,1)}, u32[]{:S(2)}, u32[]{:S(2)}) %collective-permute-start.40) | collective-permute-done | bytes 294944 | tf_op jit(solution)/shard_map/ppermute | solution.py:48
  259.7 5.5 %collective-permute-done.43 = bf16[32,4608]{1,0:T(8,128)(2,1)S(1)} collective-permute-done((bf16[32,4608]{1,0:T(8,128)(2,1)S(1)}, bf16[32,4608]{1,0:T(8,128)(2,1)S(1)}, u32[]{:S(2)}, u32[]{:S(2)}) %collective-permute-start.43) | collective-permute-done | bytes 294944 | tf_op jit(solution)/shard_map/ppermute | solution.py:48
  265.3 4.4 %collective-permute-done.42 = bf16[32,4608]{1,0:T(8,128)(2,1)S(1)} collective-permute-done((bf16[32,4608]{1,0:T(8,128)(2,1)S(1)}, bf16[32,4608]{1,0:T(8,128)(2,1)S(1)}, u32[]{:S(2)}, u32[]{:S(2)}) %collective-permute-start.42) | collective-permute-done | bytes 294944 | tf_op jit(solution)/shard_map/ppermute | solution.py:48
  269.9 4.0 %collective-permute-start.46 = (bf16[128,1024]{1,0:T(8,128)(2,1)S(1)}, bf16[128,1024]{1,0:T(8,128)(2,1)S(1)}, u32[]{:S(2)}, u32[]{:S(2)}) collective-permute-start(bf16[128,1024]{1,0:T(8,128)(2,1)S(1)} %pad_maximum_fusion.9), channel_id=1, source_target_pairs={{0,6},{1,7},{10,12},{11,13},{20,18},{21,19},{30,24},{31,25}} | collective-permute-start | bytes 786440 | tf_op jit(solution)/shard_map/ppermute | solution.py:186
  277.5 23.1 %right_pass.1.refs_0_ = bf16[7168,128]{1,0:T(8,128)(2,1)} custom-call(bf16[7168,3584]{1,0:T(8,128)(2,1)} %refs_3_.1, bf16[7168,3584]{1,0:T(8,128)(2,1)} %refs_3_.1, bf16[7168,3584]{1,0:T(8,128)(2,1)} %refs_3_.1, bf16[7168,3584]{1,0:T(8,128)(2,1)} %refs_3_.1, bf16[128,3584]{1,0:T(8,128)(2,1)} %slice.75.refs_4_), custom_call_target="tpu_custom_call" | custom-call | flops 13153337344 | bytes 51380224 | tf_op jit(solution)/shard_map/right_pass/pallas_call | solution.py:320
  306.7 3.4 collective-permute-start.49
  311.7 7.5 %collective-permute-done.48 = bf16[896,128]{1,0:T(8,128)(2,1)S(1)} collective-permute-done((bf16[896,128]{1,0:T(8,128)(2,1)S(1)}, bf16[896,128]{1,0:T(8,128)(2,1)S(1)}, u32[]{:S(2)}, u32[]{:S(2)}) %collective-permute-start.48) | collective-permute-done | bytes 229408 | tf_op jit(solution)/shard_map/ppermute | solution.py:48
  319.2 11.0 %collective-permute-done.49 = bf16[896,128]{1,0:T(8,128)(2,1)S(1)} collective-permute-done((bf16[896,128]{1,0:T(8,128)(2,1)S(1)}, bf16[896,128]{1,0:T(8,128)(2,1)S(1)}, u32[]{:S(2)}, u32[]{:S(2)}) %collective-permute-start.49) | collective-permute-done | bytes 229408 | tf_op jit(solution)/shard_map/ppermute | solution.py:48
  346.2 3.5 collective-permute-done.57
  (253 shorter events, 150.5 us)
Async XLA Ops:
  0.6 25.6 %collective-permute-start.1 = (bf16[896,256]{1,0:T(8,128)(2,1)}, bf16[896,256]{1,0:T(8,128)(2,1)}, u32[]{:S(2)}, u32[]{:S(2)}) collective-permute-start(bf16[896,256]{1,0:T(8,128)(2,1)} %param.13), channel_id=1, source_target_pairs={{0,1},{1,0},{2,3},{3,2},{4,5},{5,4},{6,7},{7,6},{8,9},{9,8},{10,11... | collective-permute-start | bytes 1376264 | tf_op jit(solution)/shard_map/ppermute | solution.py:48
  1.2 35.3 %collective-permute-start.4 = (bf16[896,256]{1,0:T(8,128)(2,1)}, bf16[896,256]{1,0:T(8,128)(2,1)S(1)}, u32[]{:S(2)}, u32[]{:S(2)}) collective-permute-start(bf16[896,256]{1,0:T(8,128)(2,1)} %param.13), channel_id=1, source_target_pairs={{0,4},{1,5},{2,6},{3,7},{4,0},{5,1},{6,2},{7,3},{8,12},{9,13},{10,... | collective-permute-start | bytes 1376264 | tf_op jit(solution)/shard_map/ppermute | solution.py:48
  4.8 21.4 %collective-permute-start.2 = (bf16[896,256]{1,0:T(8,128)(2,1)}, bf16[896,256]{1,0:T(8,128)(2,1)S(1)}, u32[]{:S(2)}, u32[]{:S(2)}) collective-permute-start(bf16[896,256]{1,0:T(8,128)(2,1)} %param.13), channel_id=1, source_target_pairs={{0,2},{1,3},{2,0},{3,1},{4,6},{5,7},{6,4},{7,5},{8,10},{9,11},{10,... | collective-permute-start | bytes 1376264 | tf_op jit(solution)/shard_map/ppermute | solution.py:48
  8.6 44.3 %collective-permute-start = (bf16[128,3584]{1,0:T(8,128)(2,1)}, bf16[128,3584]{1,0:T(8,128)(2,1)}, u32[]{:S(2)}, u32[]{:S(2)}) collective-permute-start(bf16[128,3584]{1,0:T(8,128)(2,1)} %constant_dynamic-slice_fusion.25), channel_id=1, source_target_pairs={{0,1},{1,0},{2,3},{3,2},{4,5},{5,4},{6,7},{7,6},{8,9},{9,8},{10,11... | collective-permute-start | bytes 2752520 | tf_op jit(solution)/shard_map/ppermute | solution.py:48
  13.1 43.9 %collective-permute-start.14 = (f32[1024,256]{1,0:T(8,128)}, f32[1024,256]{1,0:T(8,128)}, u32[]{:S(2)}, u32[]{:S(2)}) collective-permute-start(f32[1024,256]{1,0:T(8,128)} %constant_dynamic-slice_fusion.20), channel_id=1, source_target_pairs={{0,1},{1,0},{2,3},{3,2},{4,5},{5,4},{6,7},{7,6},{8,9},{9,8},{10,11... | collective-permute-start | bytes 3145736 | tf_op jit(solution)/shard_map/ppermute | solution.py:48
  26.3 12.6 %collective-permute-start.3 = (bf16[896,256]{1,0:T(8,128)(2,1)S(1)}, bf16[896,256]{1,0:T(8,128)(2,1)}, u32[]{:S(2)}, u32[]{:S(2)}) collective-permute-start(bf16[896,256]{1,0:T(8,128)(2,1)S(1)} %collective-permute-done.2), channel_id=1, source_target_pairs={{0,1},{1,0},{2,3},{3,2},{4,5},{5,4},{6,7},{7,6},{8,9},{9,8},{10,11... | collective-permute-start | bytes 1376264 | tf_op jit(solution)/shard_map/ppermute | solution.py:48
  37.2 14.6 %collective-permute-start.6 = (bf16[896,256]{1,0:T(8,128)(2,1)}, bf16[896,256]{1,0:T(8,128)(2,1)S(1)}, u32[]{:S(2)}, u32[]{:S(2)}) collective-permute-start(bf16[896,256]{1,0:T(8,128)(2,1)} %hold.7), channel_id=1, source_target_pairs={{0,2},{1,3},{2,0},{3,1},{4,6},{5,7},{6,4},{7,5},{8,10},{9,11},{10,... | collective-permute-start | bytes 1376264 | tf_op jit(solution)/shard_map/ppermute | solution.py:48
  38.7 17.2 %collective-permute-start.5 = (bf16[896,256]{1,0:T(8,128)(2,1)}, bf16[896,256]{1,0:T(8,128)(2,1)}, u32[]{:S(2)}, u32[]{:S(2)}) collective-permute-start(bf16[896,256]{1,0:T(8,128)(2,1)} %hold.7), channel_id=1, source_target_pairs={{0,1},{1,0},{2,3},{3,2},{4,5},{5,4},{6,7},{7,6},{8,9},{9,8},{10,11... | collective-permute-start | bytes 1376264 | tf_op jit(solution)/shard_map/ppermute | solution.py:48
  75.2 19.7 %collective-permute-start.8 = (bf16[64,3584]{1,0:T(8,128)(2,1)S(1)}, bf16[64,3584]{1,0:T(8,128)(2,1)S(1)}, u32[]{:S(2)}, u32[]{:S(2)}) collective-permute-start(bf16[64,3584]{1,0:T(8,128)(2,1)S(1)} %dynamic-slice_convert_fusion.1), channel_id=1, source_target_pairs={{0,16},{8,24},{16,0},{24,8},{1,17},{9,25},{17,1},{25,9},{2,18},{10... | collective-permute-start | bytes 1376264 | tf_op jit(solution)/shard_map/ppermute | solution.py:48
  79.8 13.5 %collective-permute-start.16 = (bf16[256,256]{1,0:T(8,128)(2,1)S(1)}, bf16[256,256]{1,0:T(8,128)(2,1)S(1)}, u32[]{:S(2)}, u32[]{:S(2)}) collective-permute-start(bf16[256,256]{1,0:T(8,128)(2,1)S(1)} %get-tuple-element.63), channel_id=1, source_target_pairs={{0,4},{1,5},{2,6},{3,7},{4,0},{5,1},{6,2},{7,3},{8,12},{9,13},{10,... | collective-permute-start | bytes 393224 | tf_op jit(solution)/shard_map/ppermute | solution.py:48
  81.9 13.2 %collective-permute-start.18 = (bf16[64,3584]{1,0:T(8,128)(2,1)S(1)}, bf16[64,3584]{1,0:T(8,128)(2,1)S(1)}, u32[]{:S(2)}, u32[]{:S(2)}) collective-permute-start(bf16[64,3584]{1,0:T(8,128)(2,1)S(1)} %dynamic-slice_convert_fusion), channel_id=1, source_target_pairs={{0,8},{8,0},{16,24},{24,16},{1,9},{9,1},{17,25},{25,17},{2,10},{10... | collective-permute-start | bytes 1376264 | tf_op jit(solution)/shard_map/ppermute | solution.py:48
  124.5 47.5 %collective-permute-start.13 = (bf16[256,896]{1,0:T(8,128)(2,1)S(1)}, bf16[256,896]{1,0:T(8,128)(2,1)S(1)}, u32[]{:S(2)}, u32[]{:S(2)}) collective-permute-start(bf16[256,896]{1,0:T(8,128)(2,1)S(1)} %get-tuple-element.24), channel_id=1, source_target_pairs={{0,2},{1,3},{2,0},{3,1},{4,6},{5,7},{6,4},{7,5},{8,10},{9,11},{10,... | collective-permute-start | bytes 1376264 | tf_op jit(solution)/shard_map/ppermute | solution.py:48
  124.6 47.4 %collective-permute-start.12 = (bf16[256,896]{1,0:T(8,128)(2,1)S(1)}, bf16[256,896]{1,0:T(8,128)(2,1)S(1)}, u32[]{:S(2)}, u32[]{:S(2)}) collective-permute-start(bf16[256,896]{1,0:T(8,128)(2,1)S(1)} %get-tuple-element.25), channel_id=1, source_target_pairs={{0,4},{1,5},{2,6},{3,7},{4,0},{5,1},{6,2},{7,3},{8,12},{9,13},{10,... | collective-permute-start | bytes 1376264 | tf_op jit(solution)/shard_map/ppermute | solution.py:48
  126.8 45.2 %collective-permute-start.11 = (bf16[256,896]{1,0:T(8,128)(2,1)S(1)}, bf16[256,896]{1,0:T(8,128)(2,1)S(1)}, u32[]{:S(2)}, u32[]{:S(2)}) collective-permute-start(bf16[256,896]{1,0:T(8,128)(2,1)S(1)} %get-tuple-element.26), channel_id=1, source_target_pairs={{0,6},{1,7},{2,4},{3,5},{4,2},{5,3},{6,0},{7,1},{8,14},{9,15},{10,... | collective-permute-start | bytes 1376264 | tf_op jit(solution)/shard_map/ppermute | solution.py:48
  202.8 27.6 %collective-permute-start.37 = (f32[4,32,32]{2,1,0:T(8,128)S(1)}, f32[4,32,32]{2,1,0:T(8,128)S(1)}, u32[]{:S(2)}, u32[]{:S(2)}) collective-permute-start(f32[4,32,32]{2,1,0:T(8,128)S(1)} %fusion.60), channel_id=1, source_target_pairs={{0,24},{8,16},{16,8},{24,0},{1,25},{9,17},{17,9},{25,1},{2,26},{10... | collective-permute-start | bytes 49160 | tf_op jit(solution)/shard_map/ppermute | solution.py:48
  204.6 25.8 %collective-permute-start.36 = (f32[4,32,32]{2,1,0:T(8,128)S(1)}, f32[4,32,32]{2,1,0:T(8,128)S(1)}, u32[]{:S(2)}, u32[]{:S(2)}) collective-permute-start(f32[4,32,32]{2,1,0:T(8,128)S(1)} %fusion.60), channel_id=1, source_target_pairs={{0,16},{8,24},{16,0},{24,8},{1,17},{9,25},{17,1},{25,9},{2,18},{10... | collective-permute-start | bytes 49160 | tf_op jit(solution)/shard_map/ppermute | solution.py:48
  205.1 25.3 %collective-permute-start.35 = (f32[4,32,32]{2,1,0:T(8,128)S(1)}, f32[4,32,32]{2,1,0:T(8,128)S(1)}, u32[]{:S(2)}, u32[]{:S(2)}) collective-permute-start(f32[4,32,32]{2,1,0:T(8,128)S(1)} %fusion.60), channel_id=1, source_target_pairs={{0,8},{8,0},{16,24},{24,16},{1,9},{9,1},{17,25},{25,17},{2,10},{10... | collective-permute-start | bytes 49160 | tf_op jit(solution)/shard_map/ppermute | solution.py:48
  239.3 14.2 %collective-permute-start.40 = (bf16[32,4608]{1,0:T(8,128)(2,1)S(1)}, bf16[32,4608]{1,0:T(8,128)(2,1)}, u32[]{:S(2)}, u32[]{:S(2)}) collective-permute-start(bf16[32,4608]{1,0:T(8,128)(2,1)S(1)} %get-tuple-element.32), channel_id=1, source_target_pairs={{0,24},{8,16},{16,8},{24,0},{1,25},{9,17},{17,9},{25,1},{2,26},{10... | collective-permute-start | bytes 884744 | tf_op jit(solution)/shard_map/ppermute | solution.py:48
  240.8 14.1 %collective-permute-start.39 = (bf16[32,4608]{1,0:T(8,128)(2,1)S(1)}, bf16[32,4608]{1,0:T(8,128)(2,1)}, u32[]{:S(2)}, u32[]{:S(2)}) collective-permute-start(bf16[32,4608]{1,0:T(8,128)(2,1)S(1)} %get-tuple-element.33), channel_id=1, source_target_pairs={{0,16},{8,24},{16,0},{24,8},{1,17},{9,25},{17,1},{25,9},{2,18},{10... | collective-permute-start | bytes 884744 | tf_op jit(solution)/shard_map/ppermute | solution.py:48
  269.9 30.7 %collective-permute-start.46 = (bf16[128,1024]{1,0:T(8,128)(2,1)S(1)}, bf16[128,1024]{1,0:T(8,128)(2,1)S(1)}, u32[]{:S(2)}, u32[]{:S(2)}) collective-permute-start(bf16[128,1024]{1,0:T(8,128)(2,1)S(1)} %pad_maximum_fusion.9), channel_id=1, source_target_pairs={{0,6},{1,7},{10,12},{11,13},{20,18},{21,19},{30,24},{31,25}} | collective-permute-start | bytes 786440 | tf_op jit(solution)/shard_map/ppermute | solution.py:186
  273.8 26.7 %collective-permute-start.45 = (bf16[128,1024]{1,0:T(8,128)(2,1)S(1)}, bf16[128,1024]{1,0:T(8,128)(2,1)S(1)}, u32[]{:S(2)}, u32[]{:S(2)}) collective-permute-start(bf16[128,1024]{1,0:T(8,128)(2,1)S(1)} %pad_maximum_fusion.9), channel_id=1, source_target_pairs={{0,4},{1,5},{10,14},{11,15},{20,16},{21,17},{30,26},{31,27}} | collective-permute-start | bytes 786440 | tf_op jit(solution)/shard_map/ppermute | solution.py:186
  275.1 25.4 %collective-permute-start.44 = (bf16[128,1024]{1,0:T(8,128)(2,1)S(1)}, bf16[128,1024]{1,0:T(8,128)(2,1)S(1)}, u32[]{:S(2)}, u32[]{:S(2)}) collective-permute-start(bf16[128,1024]{1,0:T(8,128)(2,1)S(1)} %pad_maximum_fusion.9), channel_id=1, source_target_pairs={{0,2},{1,3},{10,8},{11,9},{20,22},{21,23},{30,28},{31,29}} | collective-permute-start | bytes 786440 | tf_op jit(solution)/shard_map/ppermute | solution.py:186
  306.7 23.5 %collective-permute-start.49 = (bf16[896,128]{1,0:T(8,128)(2,1)S(1)}, bf16[896,128]{1,0:T(8,128)(2,1)S(1)}, u32[]{:S(2)}, u32[]{:S(2)}) collective-permute-start(bf16[896,128]{1,0:T(8,128)(2,1)S(1)} %get-tuple-element.38), channel_id=1, source_target_pairs={{0,4},{1,5},{2,6},{3,7},{4,0},{5,1},{6,2},{7,3},{8,12},{9,13},{10,... | collective-permute-start | bytes 688136 | tf_op jit(solution)/shard_map/ppermute | solution.py:48
  311.6 19.6 %collective-permute-start.55 = (bf16[128,1024]{1,0:T(8,128)(2,1)S(1)}, bf16[128,1024]{1,0:T(8,128)(2,1)S(1)}, u32[]{:S(2)}, u32[]{:S(2)}) collective-permute-start(bf16[128,1024]{1,0:T(8,128)(2,1)S(1)} %add_add_fusion), channel_id=1, source_target_pairs={{0,1},{1,0},{2,3},{3,2},{4,5},{5,4},{6,7},{7,6},{8,9},{9,8},{10,11... | collective-permute-start | bytes 786440 | tf_op jit(solution)/shard_map/ppermute | solution.py:48
  (64 other events, 447.5 us)
